TPU v7x, 32 devices: a whole 2x2x4 slice. The times are simulated.
32 devices in a mesh: row: 8 (over y, x, core), col: 4 (over z).
Axes of the slice: x: 2, y: 2, z: 4, core: 2. Of those that a mesh axis runs over, the one named last changes fastest.
Arguments:
- feats: bfloat16 [1024, 8192], P('col', 'row'), may hold values from -6 to 6
- w_self: bfloat16 [1024, 1024], P('col'), may hold values from -0.1875 to 0.1875
- w_neigh: bfloat16 [1024, 1024], P('col'), may hold values from -0.375 to 0.375
- cotangent: bfloat16 [1024, 8192], P('col', 'row'), may hold values from -6 to 6
- loc_nbr: int32 [8192, 8], P('row'), may hold values from 0 to 1023
- send_rows: int32 [8, 8, 128], P('row'), may hold values from 0 to 1023
- recv_node: int32 [8, 8, 128], P('row'), may hold values from -1 to 1023, as said below
- hub_rows: int32 [128], P('row'), may hold values from 0 to 1023
- hub_nbr: int32 [8192, 2], P('row'), may hold values from 0 to 127
Outputs:
- hidden_out: bfloat16 [1024, 8192], P('col', 'row')
- grad_feats: bfloat16 [1024, 8192], P('col', 'row')
- grad_self: float32 [1024, 1024], P('col')
- grad_neigh: float32 [1024, 1024], P('col')
Inputs may be any that keep to these rules, and one draw needn't show every extreme that they name: `recv_node`: for receiver block d and sender block s, the first c slots hold rows of block d and the rest hold -1, with 1 <= c <= 128; in every draw one receiver block gets all 128 slots from every sender block.
All inputs are finite; a program needn't handle non-finite values.
Results may differ from a plain program's by a relative error of at most 0.0075.
Values may be sent and summed in bfloat16 or wider, within the bound.
A program may use at most 64 MiB of HBM per device.

v0:
```python
import jax
import jax.numpy as jnp
from jax import lax
from jax.sharding import PartitionSpec as P


def silu_slope(preact):
    sigmoid_part = jax.nn.sigmoid(preact)
    return sigmoid_part * (1.0 + preact * (1.0 - sigmoid_part))


def spread_sum(values, indices, segments):
    repeats = indices.shape[1]
    spread = jnp.broadcast_to(values[:, None, :], (values.shape[0], repeats, values.shape[1]))
    return jax.ops.segment_sum(
        spread.reshape(-1, values.shape[1]).astype(jnp.float32), indices.reshape(-1), segments
    )


def per_device(feats, w_self, w_neigh, cotangent, loc_nbr, send_rows, recv_node, hub_rows, hub_nbr):
    node_rows = feats.T
    node_count, narrow = node_rows.shape
    peer_count = lax.axis_size("row")
    outgoing = feats[:, send_rows.reshape(-1)].reshape(narrow, peer_count, -1)
    incoming = lax.all_to_all(outgoing, "row", split_axis=1, concat_axis=1, tiled=True)
    hub_table = lax.all_gather(feats[:, hub_rows], "row", axis=1, tiled=True)
    targets = recv_node.reshape(-1)
    live_slots = targets >= 0
    slot_rows = jnp.where(live_slots, targets, node_count)
    local_sum = jnp.sum(node_rows[loc_nbr], axis=1, dtype=jnp.float32)
    hub_sum = jnp.sum(hub_table.T[hub_nbr], axis=1, dtype=jnp.float32)
    remote_sum = jax.ops.segment_sum(
        incoming.reshape(narrow, -1).T.astype(jnp.float32), slot_rows, node_count + 1
    )[:node_count]
    arrivals = jax.ops.segment_sum(live_slots.astype(jnp.float32), slot_rows, node_count + 1)[
        :node_count
    ]
    degree = loc_nbr.shape[1] + hub_nbr.shape[1] + arrivals
    neighbour_mean = ((local_sum + hub_sum + remote_sum) / degree[:, None]).astype(jnp.bfloat16)
    joined = jnp.concatenate([node_rows, neighbour_mean], axis=1)
    weights = jnp.concatenate([w_self, w_neigh], axis=0)
    partial_product = jnp.dot(joined, weights, preferred_element_type=jnp.float32)
    preact = lax.psum_scatter(partial_product, "col", scatter_dimension=1, tiled=True)
    hidden_out = jax.nn.silu(preact).astype(jnp.bfloat16)
    slopes = (cotangent.T.astype(jnp.float32) * silu_slope(preact)).astype(jnp.bfloat16)
    block_cols = lax.all_gather(slopes, "col", axis=1, tiled=True)
    back_sum = lax.dot_general(
        block_cols, weights, (((1,), (1,)), ((), ())), preferred_element_type=jnp.float32
    )
    weight_part = lax.dot_general(
        joined, block_cols, (((0,), (0,)), ((), ())), preferred_element_type=jnp.float32
    )
    weight_sum = weight_part
    back_sum, weight_sum = (back_sum, weight_sum)
    share_back = (back_sum[:, narrow:] / degree[:, None]).astype(jnp.bfloat16)
    hub_terms = spread_sum(share_back, hub_nbr, hub_table.shape[1])
    hub_count = hub_rows.shape[0]
    weight_total, hub_total = lax.psum((weight_sum, hub_terms), "row")
    owned_hubs = lax.dynamic_slice_in_dim(
        hub_total, lax.axis_index("row") * hub_count, hub_count, 0
    )
    share_padded = jnp.concatenate([share_back, jnp.zeros((1, narrow), jnp.bfloat16)], axis=0)
    slot_values = share_padded[slot_rows].T.reshape(narrow, peer_count, -1)
    returned = lax.all_to_all(slot_values, "row", split_axis=1, concat_axis=1, tiled=True)
    remote_grad = jax.ops.segment_sum(
        returned.reshape(narrow, -1).T.astype(jnp.float32), send_rows.reshape(-1), node_count
    )
    local_grad = spread_sum(share_back, loc_nbr, node_count)
    hub_grad = jax.ops.segment_sum(owned_hubs, hub_rows, node_count)
    grad_feats = (back_sum[:, :narrow] + local_grad + remote_grad + hub_grad).astype(jnp.bfloat16)
    return (hidden_out.T, grad_feats.T, weight_total[:narrow], weight_total[narrow:])


def solution(mesh):
    return jax.shard_map(
        per_device,
        mesh=mesh,
        in_specs=(
            P("col", "row"),
            P("col", None),
            P("col", None),
            P("col", "row"),
            P("row", None),
            P("row", None, None),
            P("row", None, None),
            P("row"),
            P("row", None),
        ),
        out_specs=(P("col", "row"), P("col", "row"), P("col", None), P("col", None)),
        check_vma=False,
    )
```

profile of v0, /device:TPU:1, one launch (start us, length us, event | category | flops | bytes accessed | tf_op | source)
XLA Modules:
  0.0 337.4 jit_solution(4424973104930199444)
XLA Ops:
  7.2 1.2 copy.19
  9.1 5.0 %gather_fusion.3 = bf16[1024,256]{1,0:T(8,128)(2,1)} fusion(bf16[256,1024]{0,1:T(8,128)(2,1)S(1)} %copy.19, s32[1024]{0:T(1024)S(1)} %broadcast_clamp_fusion.3), kind=kCustom, calls=%fused_computation.3 | custom fusion | bytes 1052672 | tf_op jit(solution)/shard_map/gather | solution.py:24
  14.1 5.4 %all-to-all-start = ((bf16[256,8,128]{0,2,1:T(8,128)(2,1)}), bf16[256,8,128]{0,2,1:T(8,128)(2,1)S(1)}, u32[]{:S(2)}, u32[]{:S(2)}) async-start(bf16[256,8,128]{0,2,1:T(8,128)(2,1)} %bitcast.9), calls=%async_computation | async-start | bytes 1048576 | tf_op jit(solution)/shard_map/all_to_all | solution.py:25
  21.2 7.6 %scatter_custom_fusion.1 = f32[1025]{0:T(1024)S(1)} fusion(s32[1024]{0:T(1024)S(1)} %bitcast.56, f32[1024]{0:T(1024)S(1)} %convert_bitcast_fusion.5, f32[]{:T(128)} %constant.13.clone.1), kind=kCustom, calls=%fused_computation.51 | custom fusion | flops 1024 | bytes 4104 | tf_op jit(solution)/shard_map/scatter-add | solution.py:35
  29.6 9.7 %all-gather = bf16[256,128]{0,1:T(8,128)(2,1)S(1)} all-gather(bf16[256,16]{0,1:T(8,128)(2,1)S(1)} %bitcast.52), channel_id=2, replica_groups=mesh['row'=8,'col'=4] {'row'}, dimensions={1}, use_global_device_ids=true | all-gather | bytes 73728 | tf_op jit(solution)/shard_map/all_gather | solution.py:26
  39.3 9.1 %gather_fusion.2 = bf16[2048,256]{1,0:T(8,128)(2,1)} fusion(bf16[128,256]{1,0:T(8,128)(2,1)S(1)} %bitcast.48, s32[2048]{0:T(1024)S(1)} %broadcast_clamp_fusion.1), kind=kCustom, calls=%fused_computation.2 | custom fusion | bytes 2105344 | tf_op jit(solution)/shard_map/gather | solution.py:31
  48.4 2.1 reshape.205
  50.5 3.7 %reduce_sum.19 = f32[1024,256]{1,0:T(8,128)} reduce(f32[1024,2,256]{2,1,0:T(2,128)S(1)} %reshape.205, f32[]{:T(128)} %constant.13.clone.1), dimensions={1}, to_apply=%region_1.2 | reduce | flops 262144 | bytes 3145732 | tf_op jit(solution)/shard_map/reduce_sum | solution.py:31
  54.2 33.1 %gather_fusion = bf16[8192,256]{1,0:T(8,128)(2,1)} fusion(bf16[1024,256]{1,0:T(8,128)(2,1)S(1)} %bitcast.45, s32[8192]{0:T(1024)S(1)} %broadcast_clamp_fusion), kind=kCustom, calls=%fused_computation | custom fusion | bytes 8421376 | tf_op jit(solution)/shard_map/gather | solution.py:30
  88.1 5.0 %convert_reduce_fusion = f32[1024,256]{1,0:T(8,128)S(1)} fusion(bf16[8192,256]{1,0:T(8,128)(2,1)} %gather_fusion), kind=kLoop, calls=%fused_computation.11 | loop fusion | flops 3932160 | bytes 5242880 | tf_op jit(solution)/shard_map/reduce_sum | solution.py:30
  93.1 7.5 %scatter_custom_fusion = f32[1025,256]{1,0:T(8,128)S(1)} fusion(s32[1024]{0:T(1024)S(1)} %bitcast.57, bf16[256,1024]{0,1:T(8,128)(2,1)S(1)} %bitcast.49, f32[]{:T(128)} %constant.13.clone.1), kind=kCustom, calls=%fused_computation.24 | custom fusion | flops 524288 | bytes 1573892 | tf_op jit(solution)/shard_map/scatter-add | solution.py:32
  100.6 1.4 fusion.5
  102.8 4.4 %fusion.10 = f32[1024,1024]{1,0:T(8,128)} fusion(bf16[512,1024]{1,0:T(8,128)(2,1)} %constant_dynamic-update-slice_fusion, bf16[1024,256]{1,0:T(8,128)(2,1)S(1)} %fusion.5, bf16[1024,256]{1,0:T(8,128)(2,1)S(1)} %bitcast.46), kind=kOutput, calls=%fused_computation.30 | convolution fusion | flops 1075838976 | bytes 6291456 | tf_op jit(solution)/shard_map/dot_general | solution.py:42
  108.5 75.7 %reduce-scatter.2.cloned.1.call-done = f32[1024,256]{1,0:T(8,128)} async-done(((f32[1024,1024]{1,0:T(8,128)}), f32[1024,256]{1,0:T(8,128)}) %reduce-scatter.2.cloned.1.call-update) | async-done | bytes 1048592 | tf_op jit(solution)/shard_map/reduce_scatter | solution.py:43
  184.2 2.6 fusion.8
  187.4 45.6 %all-gather.3.cloned.1.call-done = bf16[1024,1024]{1,0:T(8,128)(2,1)} async-done(((bf16[1024,256]{1,0:T(8,128)(2,1)}), bf16[1024,1024]{1,0:T(8,128)(2,1)}) %all-gather.3.cloned.1.call-update) | async-done | bytes 2097168 | tf_op jit(solution)/shard_map/all_gather | solution.py:46
  233.0 3.1 fusion.25
  236.2 1.6 fusion.22
  238.3 2.5 reshape.182
  240.8 12.6 %scatter_custom_fusion.4 = f32[128,256]{1,0:T(8,128)} fusion(s32[2048]{0:T(1024)S(1)} %reshape.180, f32[2048,256]{1,0:T(8,128)} %reshape.182, f32[]{:T(128)} %constant.13.clone.1), kind=kCustom, calls=%fused_computation.36 | custom fusion | flops 524288 | bytes 131584 | tf_op jit(solution)/shard_map/scatter-add | solution.py:15
  253.3 4.4 %fusion.9 = f32[512,1024]{1,0:T(8,128)} fusion(bf16[1024,1024]{1,0:T(8,128)(2,1)} %all-gather.3.cloned.1.call-done, bf16[1024,256]{1,0:T(8,128)(2,1)} %copy-done.4, bf16[1024,256]{1,0:T(8,128)(2,1)S(1)} %bitcast.47), kind=kOutput, calls=%fused_computation.29 | convolution fusion | flops 1075838976 | bytes 5242880 | tf_op jit(solution)/shard_map/dot_general | solution.py:50
  257.8 5.0 %gather_fusion.4 = bf16[1024,256]{1,0:T(8,128)(2,1)} fusion(bf16[1025,256]{1,0:T(8,128)(2,1)S(1)} %concatenate.11, s32[1024]{0:T(1024)S(1)} %get-tuple-element.24), kind=kCustom, calls=%fused_computation.4 | custom fusion | bytes 1052672 | tf_op jit(solution)/shard_map/gather | solution.py:63
  262.8 5.2 %all-to-all-start.1 = ((bf16[256,8,128]{0,2,1:T(8,128)(2,1)}), bf16[256,8,128]{0,2,1:T(8,128)(2,1)S(1)}, u32[]{:S(2)}, u32[]{:S(2)}) async-start(bf16[256,8,128]{0,2,1:T(8,128)(2,1)} %bitcast.51), calls=%async_computation.2 | async-start | bytes 1048576 | tf_op jit(solution)/shard_map/all_to_all | solution.py:64
  267.9 1.0 copy.25
  268.9 1.3 reshape.164
  270.2 1.0 copy.27
  271.2 45.3 %scatter_custom_fusion.2 = f32[1024,256]{1,0:T(8,128)S(1)} fusion(f32[1024,256]{1,0:T(8,128)S(1)} %copy-done, s32[8192]{0:T(1024)S(1)} %reshape.164, f32[1024,256]{1,0:T(8,128)S(1)} %copy-done.2), kind=kCustom, calls=%fused_computation.12 | custom fusion | flops 2097152 | bytes 2097152 | tf_op jit(solution)/shard_map/scatter-add | solution.py:15
  317.5 6.5 %scatter_custom_fusion.3 = f32[1024,256]{1,0:T(8,128)S(1)} fusion(s32[1024]{0:T(1024)} %bitcast.59, bf16[256,1024]{0,1:T(8,128)(2,1)S(1)} %bitcast.50, f32[]{:T(128)} %constant.13.clone.1), kind=kCustom, calls=%fused_computation.22 | custom fusion | flops 524288 | bytes 1573376 | tf_op jit(solution)/shard_map/scatter-add | solution.py:65
  324.0 1.4 add.103
  325.4 1.3 scatter_custom_fusion.5
  326.8 1.0 copy.28
  327.8 3.1 fusion.24
  (57 shorter events, 8.2 us)
Async XLA Ops:
  9.1 10.4 %copy-start.8 = (s32[1024,8]{0,1:T(8,128)S(1)}, s32[1024,8]{0,1:T(8,128)}, u32[]{:S(2)}) copy-start(s32[1024,8]{0,1:T(8,128)} %param.13) | copy-start | bytes 98308
  14.1 5.9 %copy-start.10 = (s32[1,8,128]{2,1,0:T(8,128)S(1)}, s32[1,8,128]{2,1,0:T(8,128)}, u32[]{:S(2)}) copy-start(s32[1,8,128]{2,1,0:T(8,128)} %param.15) | copy-start | bytes 12292
  14.1 5.9 %copy-start.11 = (s32[16]{0:T(128)S(1)}, s32[16]{0:T(128)}, u32[]{:S(2)}) copy-start(s32[16]{0:T(128)} %param.16) | copy-start | bytes 196
  14.1 6.5 %copy-start.9 = (s32[1024,2]{0,1:T(2,128)S(1)}, s32[1024,2]{0,1:T(2,128)}, u32[]{:S(2)}) copy-start(s32[1024,2]{0,1:T(2,128)} %param.17) | copy-start | bytes 24580
  14.1 14.7 %copy-start.5 = (bf16[256,1024]{1,0:T(8,128)(2,1)S(1)}, bf16[256,1024]{1,0:T(8,128)(2,1)}, u32[]{:S(2)}) copy-start(bf16[256,1024]{1,0:T(8,128)(2,1)} %param.10) | copy-start | bytes 1572868
  14.1 78.9 %all-to-all-start = ((bf16[256,8,128]{0,2,1:T(8,128)(2,1)}), bf16[256,8,128]{0,2,1:T(8,128)(2,1)S(1)}, u32[]{:S(2)}, u32[]{:S(2)}) async-start(bf16[256,8,128]{0,2,1:T(8,128)(2,1)} %bitcast.9), calls=%async_computation | async-start | bytes 1048576 | tf_op jit(solution)/shard_map/all_to_all | solution.py:25
  19.5 164.7 %reduce-scatter.2.cloned.1.call-start = ((), (), s32[]{:S(2)}) async-start(), calls=%async_computation.3 | async-start | bytes 5242880 | tf_op jit(solution)/shard_map/reduce_scatter | solution.py:43
  54.2 33.1 %copy-start.6 = (bf16[256,1024]{1,0:T(8,128)(2,1)S(1)}, bf16[256,1024]{1,0:T(8,128)(2,1)}, u32[]{:S(2)}) copy-start(bf16[256,1024]{1,0:T(8,128)(2,1)} %param.11) | copy-start | bytes 1572868
  102.0 0.8 copy-start.4
  107.2 1.0 copy-start.7
  107.3 125.7 %all-gather.3.cloned.1.call-start = ((), (), s32[]{:S(2)}) async-start(), calls=%async_computation.4 | async-start | bytes 2621440 | tf_op jit(solution)/shard_map/all_gather | solution.py:46
  186.8 138.6 %all-reduce.4.cloned.1.call-start = ((), (), s32[]{:S(2)}) async-start(), calls=%async_computation.5 | async-start | bytes 4456448 | tf_op jit(solution)/shard_map/psum | solution.py:58
  257.8 12.4 %copy-start.3 = (bf16[256,1024]{0,1:T(8,128)(2,1)S(1)}, bf16[256,1024]{0,1:T(8,128)(2,1)}, u32[]{:S(2)}) copy-start(bf16[256,1024]{0,1:T(8,128)(2,1)} %get-tuple-element.20) | copy-start | bytes 1572868
  262.8 8.5 %copy-start = (f32[1024,256]{1,0:T(8,128)S(1)}, f32[1024,256]{1,0:T(8,128)}, u32[]{:S(2)}) copy-start(f32[1024,256]{1,0:T(8,128)} %get-tuple-element.18) | copy-start | bytes 3145732
  262.8 8.5 %copy-start.2 = (f32[1024,256]{1,0:T(8,128)S(1)}, f32[1024,256]{1,0:T(8,128)}, u32[]{:S(2)}) copy-start(f32[1024,256]{1,0:T(8,128)} %get-tuple-element.14) | copy-start | bytes 3145732
  262.8 53.8 %all-to-all-start.1 = ((bf16[256,8,128]{0,2,1:T(8,128)(2,1)}), bf16[256,8,128]{0,2,1:T(8,128)(2,1)S(1)}, u32[]{:S(2)}, u32[]{:S(2)}) async-start(bf16[256,8,128]{0,2,1:T(8,128)(2,1)} %bitcast.51), calls=%async_computation.2 | async-start | bytes 1048576 | tf_op jit(solution)/shard_map/all_to_all | solution.py:64
  316.5 1.0 copy-start.1
Sparse Core Ops, SparseCore 0:
  107.4 76.7 reduce-scatter.1
  187.0 46.0 all-gather.2
  257.9 65.8 all-reduce.3
where the time goes:
time: 338 us; the launch traced here: 337 us
  waiting for transfers between devices  121 us (36%)
  other arithmetic  97.2 us (29%)
  local copies, waits for them, and re-layouts  72.3 us (21%)
  between operations  14 us (4%)
  matrix products  11.9 us (4%)
  starting transfers between devices  10.9 us (3%)
  blocking collectives  9.72 us (3%)
    reduce_scatter x1, waiting for transfers between devices, per_device(): lax.psum_scatter(partial_product, 'col', scatter_dimension=1, tiled=True)  75.7 us
    scatter-add x2, other arithmetic, spread_sum(): jax.ops.segment_sum(spread.reshape(-1, values.shape[1]).astype(jnp.float3...  57.9 us
    all_gather x1, waiting for transfers between devices, per_device(): block_cols = lax.all_gather(slopes, 'col', axis=1, tiled=True)  45.6 us
    gather x1, local copies, waits for them, and re-layouts, per_device(): local_sum = jnp.sum(node_rows[loc_nbr], axis=1, dtype=jnp.float32)  33.1 us
    all_gather x1, blocking collectives, per_device(): hub_table = lax.all_gather(feats[:, hub_rows], 'row', axis=1, tiled=True)  9.72 us
    gather x1, local copies, waits for them, and re-layouts, per_device(): hub_sum = jnp.sum(hub_table.T[hub_nbr], axis=1, dtype=jnp.float32)  9.05 us
    unnamed x31, local copies, waits for them, and re-layouts  8.05 us
    scatter-add x1, other arithmetic, per_device(): jax.ops.segment_sum(live_slots.astype(jnp.float32), slot_rows, node_count...  7.57 us
  transfers between devices with their start and end apart: 5, of which 2 were waited for; matrix products, arithmetic and copies ran while one was open for 37% of the time, Pallas kernels for 0%

commit v1 on v0

v1 whole, which is shorter than its diff:
```python
import jax
import jax.numpy as jnp
from jax import lax
from jax.sharding import PartitionSpec as P

BF16 = jnp.bfloat16
F32 = jnp.float32


def silu_slope(preact):
    sigmoid_part = jax.nn.sigmoid(preact)
    return sigmoid_part * (1.0 + preact * (1.0 - sigmoid_part))


def dot(a, b, ca, cb):
    return lax.dot_general(a, b, (((ca,), (cb,)), ((), ())), preferred_element_type=F32)


def picks(indices, size):
    rows = lax.broadcasted_iota(jnp.int32, (size, indices.shape[1]), 0)
    total = (rows == indices[0:1]).astype(F32)
    for k in range(1, indices.shape[0]):
        total = total + (rows == indices[k : k + 1]).astype(F32)
    return total.astype(BF16)


def per_device(feats, w_self, w_neigh, cotangent, loc_nbr, send_rows, recv_node, hub_rows, hub_nbr):
    narrow, nodes = feats.shape
    peers = lax.axis_size("row")
    send_pick = picks(send_rows.reshape(1, -1), nodes)
    recv_pick = picks(recv_node.reshape(1, -1), nodes)
    loc_pick = picks(loc_nbr.T, nodes)
    hub_pick = picks(hub_nbr.T, peers * hub_rows.shape[0])
    own_pick = picks(hub_rows.reshape(1, -1), nodes)

    outgoing = dot(feats, send_pick, 1, 0).astype(BF16).reshape(narrow, peers, -1)
    incoming = lax.all_to_all(outgoing, "row", split_axis=1, concat_axis=1, tiled=True)
    hub_table = lax.all_gather(dot(own_pick, feats, 0, 1).astype(BF16), "row", axis=0, tiled=True)
    arrivals = jnp.sum((recv_pick).astype(F32), axis=1)
    degree = (loc_nbr.shape[1] + hub_nbr.shape[1] + arrivals)[None, :]
    total = dot(feats, loc_pick, 1, 0) + dot(hub_table, hub_pick, 0, 0)
    total = total + dot(incoming.reshape(narrow, -1), recv_pick, 1, 1)
    agg = (total / degree).astype(BF16)
    joined = jnp.concatenate([feats, agg], axis=0)
    weights = jnp.concatenate([w_self, w_neigh], axis=0)
    partial = dot(weights, joined, 0, 0).astype(BF16)
    preact = lax.psum_scatter(partial, "col", scatter_dimension=0, tiled=True).astype(F32)
    hidden_out = jax.nn.silu(preact).astype(BF16)
    slopes = (cotangent.astype(F32) * silu_slope(preact)).astype(BF16)
    wide = lax.all_gather(slopes, "col", axis=0, tiled=True)
    back = dot(weights, wide, 1, 0)
    share = (back[narrow:] / degree).astype(BF16)
    weight_total = lax.psum(dot(joined, wide, 1, 1), "row")
    hub_part = dot(hub_pick, share, 1, 1)
    owned = lax.psum_scatter(hub_part, "row", scatter_dimension=0, tiled=True)
    high = owned.astype(BF16)
    low = (owned - high.astype(F32)).astype(BF16)
    slot_values = dot(share, recv_pick, 1, 0).astype(BF16).reshape(narrow, peers, -1)
    returned = lax.all_to_all(slot_values, "row", split_axis=1, concat_axis=1, tiled=True)
    grad = back[:narrow] + dot(share, loc_pick, 1, 1)
    grad = grad + dot(high, own_pick, 0, 1) + dot(low, own_pick, 0, 1)
    grad = grad + dot(returned.reshape(narrow, -1), send_pick, 1, 1)
    return hidden_out, grad.astype(BF16), weight_total[:narrow], weight_total[narrow:]


def solution(mesh):
    return jax.shard_map(
        per_device,
        mesh=mesh,
        in_specs=(
            P("col", "row"),
            P("col", None),
            P("col", None),
            P("col", "row"),
            P("row", None),
            P("row", None, None),
            P("row", None, None),
            P("row"),
            P("row", None),
        ),
        out_specs=(P("col", "row"), P("col", "row"), P("col", None), P("col", None)),
        check_vma=False,
    )
```

time: 338 us -> 242 us (0.72)
  other arithmetic: 97.2 us -> 3.12 us
  local copies, waits for them, and re-layouts: 72.3 us -> 6.57 us
  waiting for transfers between devices: 121 us -> 166 us
  matrix products: 11.9 us -> 28.3 us
    scatter-add x6 -> x0, other arithmetic: 80.7 us -> none  [the longest x2 57.9 us: spread_sum(): jax.ops.segment_sum(spread.reshape(-1, values.shape[1]).astype(jnp.float3...]
    psum x1, waiting for transfers between devices: 0.02 us -> 60.6 us  [per_device(): weight_total = lax.psum(dot(joined, wide, 1, 1), 'row')]
    gather x5 -> x0, local copies, waits for them, and re-layouts: 52.7 us -> none  [the longest x1 33.1 us: per_device(): local_sum = jnp.sum(node_rows[loc_nbr], axis=1, dtype=jnp.float32)]
    reduce_scatter x1 -> x2, waiting for transfers between devices: 75.7 us -> 59.3 us  [the longest x1 43.6 us: per_device(): lax.psum_scatter(partial, 'col', scatter_dimension=0, tiled=True)]
    dot_general x3 -> x14, matrix products: 11.9 us -> 28.3 us  [dot(): lax.dot_general(a, b, (((ca,), (cb,)), ((), ())), preferred_element_type=...]
    reduce_sum x2 -> x1, other arithmetic: 8.65 us -> 0.49 us  [per_device(): arrivals = jnp.sum(recv_pick.astype(F32), axis=1)]
    unnamed x31 -> x27, local copies, waits for them, and re-layouts: 8.05 us -> 2.3 us
    convert_element_type x2 -> x0, local copies, waits for them, and re-layouts: 4.57 us -> none  [the longest x1 2.49 us: spread_sum(): spread.reshape(-1, values.shape[1]).astype(jnp.float32)]
  transfers between devices with their start and end apart: 5 -> 6, of which waited for: 2 -> 4; matrix products, arithmetic and copies ran while one was open for 37% -> 8% of each run, Pallas kernels for 0% -> 0%
where the time goes in v1:
time: 242 us; the launch traced here: 240 us
  waiting for transfers between devices  166 us (69%)
  matrix products  28.3 us (12%)
  between operations  14 us (6%)
  blocking collectives  12.7 us (5%)
  starting transfers between devices  9.98 us (4%)
  local copies, waits for them, and re-layouts  6.57 us (3%)
  other arithmetic  3.12 us (1%)
    psum x1, waiting for transfers between devices, per_device(): weight_total = lax.psum(dot(joined, wide, 1, 1), 'row')  60.6 us
    all_gather x1, waiting for transfers between devices, per_device(): wide = lax.all_gather(slopes, 'col', axis=0, tiled=True)  45.5 us
    reduce_scatter x1, waiting for transfers between devices, per_device(): lax.psum_scatter(partial, 'col', scatter_dimension=0, tiled=True)  43.6 us
    dot_general x14, matrix products, dot(): lax.dot_general(a, b, (((ca,), (cb,)), ((), ())), preferred_element_type=...  28.3 us
    reduce_scatter x1, waiting for transfers between devices, per_device(): owned = lax.psum_scatter(hub_part, 'row', scatter_dimension=0, tiled=True)  15.7 us
    all_gather x1, blocking collectives, per_device(): lax.all_gather(dot(own_pick, feats, 0, 1).astype(BF16), 'row', axis=0, ti...  12.7 us
    all_to_all x1, starting transfers between devices, per_device(): lax.all_to_all(outgoing, 'row', split_axis=1, concat_axis=1, tiled=True)  5.37 us
  transfers between devices with their start and end apart: 6, of which 4 were waited for; matrix products, arithmetic and copies ran while one was open for 8% of the time, Pallas kernels for 0%

profile of v1, /device:TPU:1, one launch (start us, length us, event | category | flops | bytes accessed | tf_op | source)
XLA Modules:
  0.0 240.1 jit_solution(4946758894678773947)
XLA Ops:
  7.2 2.7 %fusion.11 = bf16[1024,256]{1,0:T(8,128)(2,1)} fusion(bf16[256,1024]{1,0:T(8,128)(2,1)} %param.9, s32[1024]{0:T(1024)} %bitcast.66), kind=kOutput, calls=%fused_computation.34 | convolution fusion | flops 540278784 | bytes 1052672 | tf_op jit(solution)/shard_map/dot_general | solution.py:16
  9.9 5.4 %all-to-all-start = ((bf16[256,8,128]{0,2,1:T(8,128)(2,1)}), bf16[256,8,128]{0,2,1:T(8,128)(2,1)S(1)}, u32[]{:S(2)}, u32[]{:S(2)}) async-start(bf16[256,8,128]{0,2,1:T(8,128)(2,1)} %bitcast.15), calls=%async_computation | async-start | bytes 1048576 | tf_op jit(solution)/shard_map/all_to_all | solution.py:37
  15.4 0.2 convolution_convert_fusion.1
  15.6 12.7 %all_gather.6 = bf16[128,256]{1,0:T(8,128)(2,1)S(1)} all-gather(bf16[16,256]{1,0:T(8,128)(2,1)S(1)} %convolution_convert_fusion.1), channel_id=1, replica_groups=mesh['row'=8,'col'=4] {'row'}, dimensions={0}, use_global_device_ids=true | all-gather | bytes 73728 | tf_op jit(solution)/shard_map/all_gather | solution.py:38
  28.3 0.5 convert_reduce_fusion
  28.8 4.2 %convolution_bitcast_fusion = f32[256,1024]{1,0:T(8,128)S(1)} fusion(bf16[256,1024]{1,0:T(8,128)(2,1)S(1)} %copy-done.1, s32[1024]{0:T(1024)S(1)} %bitcast.49, s32[1024]{0:T(1024)S(1)} %bitcast.51, s32[1024]{0:T(1024)S(1)} %bitcast.53, s32[1024]{0:T(1024)S(1)} %bitcast.55, s32[1024]{0:T(1024)S(1)} %bitcast.57, s32[1024]{0:T(1024)S(1)} %bitcast.59, ...), kind=kOutput, calls=%fused_computation.26 | convolution fusion | flops 562036736 | bytes 1605632 | tf_op jit(solution)/shard_map/dot_general | solution.py:16
  33.1 0.3 convolution_add_fusion.2
  33.4 0.8 fusion.14
  34.2 0.8 copy-done.11
  35.0 2.6 %convolution_convert_fusion = bf16[1024,1024]{1,0:T(8,128)(2,1)} fusion(bf16[512,1024]{1,0:T(8,128)(2,1)S(1)} %constant_dynamic-update-slice_fusion, bf16[256,1024]{1,0:T(8,128)(2,1)S(1)} %fusion.14, bf16[256,1024]{1,0:T(8,128)(2,1)S(1)} %copy-done.1), kind=kOutput, calls=%fused_computation.22 | convolution fusion | flops 1076887552 | bytes 4194304 | tf_op jit(solution)/shard_map/dot_general | solution.py:16
  37.6 0.0 all-gather.2.cloned.1.call-start
  37.7 43.6 %reduce-scatter.3.cloned.1.call-done = bf16[256,1024]{1,0:T(8,128)(2,1)} async-done(((bf16[1024,1024]{1,0:T(8,128)(2,1)}), bf16[256,1024]{1,0:T(8,128)(2,1)}) %reduce-scatter.3.cloned.1.call-update) | async-done | bytes 524304 | tf_op jit(solution)/shard_map/reduce_scatter | solution.py:47
  81.3 2.5 %fusion.23 = (bf16[256,1024]{1,0:T(8,128)(2,1)}, bf16[256,1024]{1,0:T(8,128)(2,1)}) fusion(bf16[256,1024]{1,0:T(8,128)(2,1)} %reduce-scatter.3.cloned.1.call-done, bf16[256,1024]{1,0:T(8,128)(2,1)S(1)} %copy-done.4), kind=kLoop, calls=%fused_computation.47 | loop fusion | flops 3407872 | bytes 2097152 | tf_op jit(solution)/shard_map/convert_element_type | solution.py:49
  83.9 45.5 %all-gather.2.cloned.1.call-done = bf16[1024,1024]{1,0:T(8,128)(2,1)} async-done(((bf16[256,1024]{1,0:T(8,128)(2,1)}), bf16[1024,1024]{1,0:T(8,128)(2,1)}) %all-gather.2.cloned.1.call-update) | async-done | bytes 2097168 | tf_op jit(solution)/shard_map/all_gather | solution.py:50
  129.4 2.8 %fusion.41 = f32[512,1024]{1,0:T(8,128)S(1)} fusion(bf16[512,1024]{1,0:T(8,128)(2,1)S(1)} %constant_dynamic-update-slice_fusion, bf16[1024,1024]{1,0:T(8,128)(2,1)} %all-gather.2.cloned.1.call-done), kind=kOutput, calls=%fused_computation.77 | convolution fusion | flops 1073741824 | bytes 5242880 | tf_op jit(solution)/shard_map/dot_general | solution.py:16
  132.3 1.3 copy-done
  133.6 0.1 fusion.24
  133.7 1.0 fusion.26
  134.7 0.2 all-reduce.2.cloned.1.call-start
  134.9 4.2 %fusion.25 = f32[512,1024]{1,0:T(8,128)} fusion(bf16[1024,1024]{1,0:T(8,128)(2,1)} %all-gather.2.cloned.1.call-done, bf16[256,1024]{1,0:T(8,128)(2,1)S(1)} %copy-done.12, bf16[256,1024]{1,0:T(8,128)(2,1)S(1)} %copy-done.1), kind=kOutput, calls=%fused_computation.51 | convolution fusion | flops 1075838976 | bytes 5242880 | tf_op jit(solution)/shard_map/dot_general | solution.py:16
  139.1 5.7 %convolution_add_fusion.3 = f32[256,1024]{1,0:T(8,128)S(1)} fusion(bf16[256,1024]{1,0:T(8,128)(2,1)S(1)} %fusion.24, f32[512,1024]{1,0:T(8,128)} %copy-done, s32[1024]{0:T(1024)S(1)} %bitcast.50, s32[1024]{0:T(1024)S(1)} %bitcast.52, s32[1024]{0:T(1024)S(1)} %bitcast.54, s32[1024]{0:T(1024)S(1)} %bitcast.56, s32[1024]{0:T(1024)S(1)} %bitcast.58, ...), kind=kOutput, calls=%fused_computation.32 | convolution fusion | flops 562298880 | bytes 2654208 | tf_op jit(solution)/shard_map/dot_general | solution.py:16
  144.8 0.7 fusion.15
  145.6 0.9 copy.20
  146.5 4.3 %all-to-all-start.1 = ((bf16[256,8,128]{2,0,1:T(8,128)(2,1)}), bf16[256,8,128]{2,0,1:T(8,128)(2,1)S(1)}, u32[]{:S(2)}, u32[]{:S(2)}) async-start(bf16[256,8,128]{2,0,1:T(8,128)(2,1)} %bitcast.38), calls=%async_computation.3 | async-start | bytes 1048576 | tf_op jit(solution)/shard_map/all_to_all | solution.py:59
  150.8 15.7 %reduce-scatter.5.cloned.1.call-done = f32[16,256]{1,0:T(8,128)} async-done(((f32[128,256]{1,0:T(8,128)}), f32[16,256]{1,0:T(8,128)}) %reduce-scatter.5.cloned.1.call-update) | async-done | bytes 16400 | tf_op jit(solution)/shard_map/reduce_scatter | solution.py:55
  166.5 1.1 convolution_add_fusion.1
  167.6 0.3 convolution_add_fusion
  168.0 0.2 copy.17
  168.2 0.1 copy-done.10
  168.3 1.6 fusion.10
  169.8 60.6 %all-reduce.2.cloned.1.call-done = f32[512,1024]{1,0:T(8,128)} async-done(((f32[512,1024]{1,0:T(8,128)}), f32[512,1024]{1,0:T(8,128)}) %all-reduce.2.cloned.1.call-update) | async-done | bytes 2097168 | tf_op jit(solution)/shard_map/psum | solution.py:53
  230.5 3.1 %fusion.38 = (f32[256,1024]{1,0:T(8,128)}, f32[256,1024]{1,0:T(8,128)}) fusion(f32[512,1024]{1,0:T(8,128)} %all-reduce.2.cloned.1.call-done), kind=kLoop, calls=%fused_computation.74 | loop fusion | bytes 4194304 | tf_op jit(solution)/shard_map/slice | solution.py:63
  (36 shorter events, 0.3 us)
Async XLA Ops:
  7.2 8.1 %copy-start.2 = (bf16[256,1024]{1,0:T(8,128)(2,1)S(1)}, bf16[256,1024]{1,0:T(8,128)(2,1)}, u32[]{:S(2)}) copy-start(bf16[256,1024]{1,0:T(8,128)(2,1)} %param.10) | copy-start | bytes 1572868
  9.9 5.5 %copy-start.6 = (s32[1024,8]{0,1:T(8,128)S(1)}, s32[1024,8]{0,1:T(8,128)}, u32[]{:S(2)}) copy-start(s32[1024,8]{0,1:T(8,128)} %param.13) | copy-start | bytes 98308
  9.9 5.5 %copy-start.1 = (bf16[256,1024]{1,0:T(8,128)(2,1)S(1)}, bf16[256,1024]{1,0:T(8,128)(2,1)}, u32[]{:S(2)}) copy-start(bf16[256,1024]{1,0:T(8,128)(2,1)} %param.9) | copy-start | bytes 1572868
  9.9 5.5 %copy-start.8 = (s32[16]{0:T(128)S(1)}, s32[16]{0:T(128)}, u32[]{:S(2)}) copy-start(s32[16]{0:T(128)} %param.16) | copy-start | bytes 196
  9.9 18.4 %copy-start.7 = (s32[1024,2]{0,1:T(2,128)S(1)}, s32[1024,2]{0,1:T(2,128)}, u32[]{:S(2)}) copy-start(s32[1024,2]{0,1:T(2,128)} %param.17) | copy-start | bytes 24580
  9.9 18.4 %copy-start.9 = (s32[1,8,128]{2,1,0:T(8,128)S(1)}, s32[1,8,128]{2,1,0:T(8,128)}, u32[]{:S(2)}) copy-start(s32[1,8,128]{2,1,0:T(8,128)} %param.15) | copy-start | bytes 12292
  9.9 18.9 %copy-start.3 = (bf16[256,1024]{1,0:T(8,128)(2,1)S(1)}, bf16[256,1024]{1,0:T(8,128)(2,1)}, u32[]{:S(2)}) copy-start(bf16[256,1024]{1,0:T(8,128)(2,1)} %param.11) | copy-start | bytes 1572868
  9.9 23.5 %all-to-all-start = ((bf16[256,8,128]{0,2,1:T(8,128)(2,1)}), bf16[256,8,128]{0,2,1:T(8,128)(2,1)S(1)}, u32[]{:S(2)}, u32[]{:S(2)}) async-start(bf16[256,8,128]{0,2,1:T(8,128)(2,1)} %bitcast.15), calls=%async_computation | async-start | bytes 1048576 | tf_op jit(solution)/shard_map/all_to_all | solution.py:37
  15.3 66.0 %reduce-scatter.3.cloned.1.call-start = ((), (), s32[]{:S(2)}) async-start(), calls=%async_computation.4 | async-start | bytes 2621440 | tf_op jit(solution)/shard_map/reduce_scatter | solution.py:47
  34.2 0.8 copy-start.11
  37.6 43.7 %copy-start.4 = (bf16[256,1024]{1,0:T(8,128)(2,1)S(1)}, bf16[256,1024]{1,0:T(8,128)(2,1)}, u32[]{:S(2)}) copy-start(bf16[256,1024]{1,0:T(8,128)(2,1)} %param.12) | copy-start | bytes 1572868
  37.6 91.8 %all-gather.2.cloned.1.call-start = ((), (), s32[]{:S(2)}) async-start(), calls=%async_computation.5 | async-start | bytes 2621440 | tf_op jit(solution)/shard_map/all_gather | solution.py:50
  83.8 82.6 %reduce-scatter.5.cloned.1.call-start = ((), (), s32[]{:S(2)}) async-start(), calls=%async_computation.6 | async-start | bytes 147456 | tf_op jit(solution)/shard_map/reduce_scatter | solution.py:55
  132.2 1.3 copy-start
  133.6 1.4 copy-start.12
  134.7 95.8 %all-reduce.2.cloned.1.call-start = ((), (), s32[]{:S(2)}) async-start(), calls=%async_computation.7 | async-start | bytes 4194304 | tf_op jit(solution)/shard_map/psum | solution.py:53
  146.5 21.5 %all-to-all-start.1 = ((bf16[256,8,128]{2,0,1:T(8,128)(2,1)}), bf16[256,8,128]{2,0,1:T(8,128)(2,1)S(1)}, u32[]{:S(2)}, u32[]{:S(2)}) async-start(bf16[256,8,128]{2,0,1:T(8,128)(2,1)} %bitcast.38), calls=%async_computation.3 | async-start | bytes 1048576 | tf_op jit(solution)/shard_map/all_to_all | solution.py:59
  166.5 1.1 copy-start.5
  167.6 0.7 copy-start.10
Sparse Core Ops, SparseCore 0:
  37.7 43.4 reduce-scatter.2
  83.9 45.4 all-gather.1
  134.8 31.5 reduce-scatter.4
  169.5 60.8 all-reduce.1

commit v2 on v1

v2 whole, which is shorter than its diff:
```python
import functools

import jax
import jax.numpy as jnp
from jax import lax
from jax.experimental import pallas as pl
from jax.experimental.pallas import tpu as pltpu
from jax.sharding import PartitionSpec as P

BF16 = jnp.bfloat16
F32 = jnp.float32
MESH = pl.DeviceIdType.MESH


def dot(a, b, ca, cb):
    return lax.dot_general(a, b, (((ca,), (cb,)), ((), ())), preferred_element_type=F32)


def fill_picks(dest, indices, strip):
    size = dest.shape[0]
    strip = min(strip, size)

    def body(i, carry):
        first = pl.multiple_of(i * strip, strip)
        rows = lax.broadcasted_iota(jnp.int32, (strip, indices.shape[1]), 0) + first
        total = jnp.where(rows == indices[0:1, :], 1.0, 0.0)
        for k in range(1, indices.shape[0]):
            total = total + jnp.where(rows == indices[k : k + 1, :], 1.0, 0.0)
        dest[pl.ds(first, strip), :] = total.astype(BF16)
        return carry

    lax.fori_loop(0, size // strip, body, 0)


def layer_kernel(
    n, peers, chunks,
    feats, w_self, w_neigh, w_turned, cot, loc, send, recv, hub_col, hub,
    hidden, grad_feats, grad_self, grad_neigh,
    loc_pick, send_pick, recv_pick, hub_pick, own_pick, degree,
    slot_out, slot_in, hub_out, hub_in,
    total, joined, from_left, from_right, to_left, to_right, slopes,
    direct, share, weight_acc, weight_out, weight_in, weight_sum, weight_all,
    back_out, back_in, hub_back_out, hub_back_in,
    row_send, row_recv, sum_send, sum_recv, spread_send, spread_recv,
):
    narrow, nodes = feats.shape
    width = nodes // chunks
    slots = send.shape[1] // peers
    hubs = hub_col.shape[0]
    me = lax.axis_index("row")
    pos = lax.axis_index("col")
    has_left = pos > 0
    has_right = pos < n - 1

    def row_peer(d):
        return lax.rem(me + d, peers)

    def row_source(d):
        return lax.rem(me + peers - d, peers)

    barrier = pltpu.get_barrier_semaphore()
    for d in range(1, peers):
        pl.semaphore_signal(barrier, inc=1, device_id={"row": row_peer(d)}, device_id_type=MESH)

    @pl.when(has_left)
    def _():
        pl.semaphore_signal(barrier, inc=1, device_id={"col": pos - 1}, device_id_type=MESH)

    @pl.when(has_right)
    def _():
        pl.semaphore_signal(barrier, inc=1, device_id={"col": pos + 1}, device_id_type=MESH)

    def cols(index, size):
        return pl.ds(pl.multiple_of(index * size, size), size)

    def row_copy(src, dst, kind, d):
        return pltpu.make_async_remote_copy(
            src_ref=src, dst_ref=dst, send_sem=row_send.at[kind, d], recv_sem=row_recv.at[kind, d],
            device_id={"row": row_peer(d)}, device_id_type=MESH,
        )

    def slot_copy(d):
        return row_copy(slot_out.at[:, cols(row_peer(d), slots)], slot_in.at[:, cols(me, slots)], 0, d)

    def hub_copy(d):
        return row_copy(hub_out, hub_in.at[cols(me, hubs), :], 1, d)

    def back_copy(d):
        return row_copy(back_out.at[:, cols(row_peer(d), slots)], back_in.at[:, cols(me, slots)], 2, d)

    def hub_back_copy(d):
        return row_copy(hub_back_out.at[cols(row_peer(d), hubs), :], hub_back_in.at[me], 3, d)

    lane_parts = min(peers, weight_acc.shape[1] // 128)
    row_parts = peers // lane_parts
    part_rows = weight_acc.shape[0] // row_parts
    part_cols = weight_acc.shape[1] // lane_parts

    def part(r):
        return cols(lax.div(r, lane_parts), part_rows), cols(lax.rem(r, lane_parts), part_cols)

    def weight_copy(d):
        rows, columns = part(row_peer(d))
        return row_copy(weight_out.at[rows, columns], weight_in.at[me], 4, d)

    def weight_share(d):
        rows, columns = part(me)
        return row_copy(weight_sum, weight_all.at[rows, columns], 5, d)

    fill_picks(send_pick, send, 64)
    own_rows = lax.broadcasted_iota(jnp.int32, (hubs, nodes), 1)
    own_pick[...] = jnp.where(own_rows == hub_col[...], 1.0, 0.0).astype(BF16)
    hub_out[...] = dot(own_pick[...], feats[...], 1, 1).astype(BF16)

    tile = 2 * slots

    def gather_out(i, carry):
        slot_out[:, cols(i, tile)] = dot(feats[...], send_pick[:, cols(i, tile)], 1, 0).astype(BF16)
        return carry

    lax.fori_loop(0, peers * slots // tile, gather_out, 0)

    pl.semaphore_wait(barrier, peers - 1 + has_left.astype(jnp.int32) + has_right.astype(jnp.int32))
    for d in range(1, peers):
        slot_copy(d).start()
        hub_copy(d).start()
    slot_in[:, cols(me, slots)] = slot_out[:, cols(me, slots)]
    hub_in[cols(me, hubs), :] = hub_out[...]

    fill_picks(loc_pick, loc, 64)
    fill_picks(recv_pick, recv, 64)
    fill_picks(hub_pick, hub, 64)
    fixed = loc.shape[0] + hub.shape[0]

    def local_part(k, carry):
        total[k] = dot(feats[...], loc_pick[:, cols(k, width)], 1, 0)
        joined[k, 0:narrow, :] = feats[:, cols(k, width)]
        ones = jnp.ones((16, recv_pick.shape[1]), BF16)
        degree[k] = dot(ones, recv_pick[cols(k, width), :], 1, 1) + fixed
        return carry

    lax.fori_loop(0, chunks, local_part, 0)
    weight_acc[...] = jnp.zeros_like(weight_acc)
    for d in range(1, peers):
        slot_copy(d).wait_recv()
        hub_copy(d).wait_recv()

    def right_copy(owner, k):
        return pltpu.make_async_remote_copy(
            src_ref=to_right.at[k, owner], dst_ref=from_left.at[k, owner],
            send_sem=sum_send.at[0, k, owner], recv_sem=sum_recv.at[0, k, owner],
            device_id={"col": pos + 1}, device_id_type=MESH,
        )

    def left_copy(owner, k):
        return pltpu.make_async_remote_copy(
            src_ref=to_left.at[k, owner], dst_ref=from_right.at[k, owner],
            send_sem=sum_send.at[1, k, owner], recv_sem=sum_recv.at[1, k, owner],
            device_id={"col": pos - 1}, device_id_type=MESH,
        )

    def slopes_right(owner, k):
        return pltpu.make_async_remote_copy(
            src_ref=slopes.at[k, owner], dst_ref=slopes.at[k, owner],
            send_sem=spread_send.at[0, k, owner], recv_sem=spread_recv.at[0, k, owner],
            device_id={"col": pos + 1}, device_id_type=MESH,
        )

    def slopes_left(owner, k):
        return pltpu.make_async_remote_copy(
            src_ref=slopes.at[k, owner], dst_ref=slopes.at[k, owner],
            send_sem=spread_send.at[1, k, owner], recv_sem=spread_recv.at[1, k, owner],
            device_id={"col": pos - 1}, device_id_type=MESH,
        )

    def send_partials(k):
        mean = total[k] + dot(hub_in[...], hub_pick[:, cols(k, width)], 0, 0)
        mean = mean + dot(slot_in[...], recv_pick[cols(k, width), :], 1, 1)
        joined[k, narrow:, :] = (mean / degree[k, 0:1, :]).astype(BF16)

        def step(s, carry):
            far = n - 1 - s

            @pl.when(far > pos)
            def _():
                mine = dot(w_turned[far], joined[k], 1, 0)

                @pl.when(has_left)
                def _():
                    right_copy(far, k).wait_recv()
                    to_right[k, far] = (mine + from_left[k, far].astype(F32)).astype(BF16)

                @pl.when(jnp.logical_not(has_left))
                def _():
                    to_right[k, far] = mine.astype(BF16)

                right_copy(far, k).start()

            @pl.when(s < pos)
            def _():
                mine = dot(w_turned[s], joined[k], 1, 0)

                @pl.when(has_right)
                def _():
                    left_copy(s, k).wait_recv()
                    to_left[k, s] = (mine + from_right[k, s].astype(F32)).astype(BF16)

                @pl.when(jnp.logical_not(has_right))
                def _():
                    to_left[k, s] = mine.astype(BF16)

                left_copy(s, k).start()

            return carry

        lax.fori_loop(0, n - 1, step, 0)

    def finish_preact(k):
        total[k] = dot(w_turned[pos], joined[k], 1, 0)

        @pl.when(has_left)
        def _():
            right_copy(pos, k).wait_recv()
            total[k] = total[k] + from_left[k, pos].astype(F32)

        @pl.when(has_right)
        def _():
            left_copy(pos, k).wait_recv()
            total[k] = total[k] + from_right[k, pos].astype(F32)

        preact = total[k]
        gate = jax.nn.sigmoid(preact)
        slope = gate * (1.0 + preact * (1.0 - gate))
        slopes[k, pos] = (cot[:, cols(k, width)].astype(F32) * slope).astype(BF16)

        @pl.when(has_right)
        def _():
            slopes_right(pos, k).start()

        @pl.when(has_left)
        def _():
            slopes_left(pos, k).start()

        hidden[:, cols(k, width)] = (preact * gate).astype(BF16)

    def backward(k):
        def step(d, carry):
            @pl.when(pos - d >= 0)
            def _():
                slopes_right(pos - d, k).wait_recv()

                @pl.when(has_right)
                def _():
                    slopes_right(pos - d, k).start()

            @pl.when(pos + d < n)
            def _():
                slopes_left(pos + d, k).wait_recv()

                @pl.when(has_left)
                def _():
                    slopes_left(pos + d, k).start()

            return carry

        lax.fori_loop(1, n, step, 0)
        wide = slopes[k].reshape(n * narrow, width)
        back = dot(w_neigh[...], wide, 1, 0)
        share[:, cols(k, width)] = (back / degree[k, 0:1, :]).astype(BF16)
        direct[k] = dot(w_self[...], wide, 1, 0)
        weight_acc[...] += dot(joined[k], wide, 1, 1)

    def turn(t, carry):
        @pl.when(t < chunks)
        def _():
            send_partials(t)

        @pl.when(jnp.logical_and(t >= 1, t <= chunks))
        def _():
            finish_preact(t - 1)

        @pl.when(t >= 2)
        def _():
            backward(t - 2)

        return carry

    lax.fori_loop(0, chunks + 2, turn, 0)

    def back_slots(i, carry):
        back_out[:, cols(i, tile)] = dot(share[...], recv_pick[:, cols(i, tile)], 1, 0).astype(BF16)
        return carry

    lax.fori_loop(0, peers * slots // tile, back_slots, 0)
    hub_back_out[...] = dot(hub_pick[...], share[...], 1, 1)
    for d in range(1, peers):
        back_copy(d).start()
        hub_back_copy(d).start()
    weight_out[...] = weight_acc[...].astype(BF16)
    for d in range(1, peers):
        weight_copy(d).start()
    back_in[:, cols(me, slots)] = back_out[:, cols(me, slots)]
    hub_back_in[me] = hub_back_out[cols(me, hubs), :]
    my_rows, my_cols = part(me)
    weight_in[me] = weight_out[my_rows, my_cols]

    def local_back(k, carry):
        direct[k] = direct[k] + dot(share[...], loc_pick[cols(k, width), :], 1, 1)
        return carry

    lax.fori_loop(0, chunks, local_back, 0)
    for d in range(1, peers):
        back_copy(d).wait_recv()
        hub_back_copy(d).wait_recv()
    hub_total = hub_back_in[0]
    for r in range(1, peers):
        hub_total = hub_total + hub_back_in[r]
    hub_high = hub_total.astype(BF16)
    hub_low = (hub_total - hub_high.astype(F32)).astype(BF16)

    for d in range(1, peers):
        weight_copy(d).wait_recv()
    sums = weight_in[0].astype(F32)
    for r in range(1, peers):
        sums = sums + weight_in[r].astype(F32)
    weight_sum[...] = sums.astype(BF16)
    for d in range(1, peers):
        weight_share(d).start()
    weight_all[my_rows, my_cols] = weight_sum[...]

    def finish_grad(k, carry):
        grad = direct[k] + dot(back_in[...], send_pick[cols(k, width), :], 1, 1)
        grad = grad + dot(hub_high, own_pick[:, cols(k, width)], 0, 0)
        grad = grad + dot(hub_low, own_pick[:, cols(k, width)], 0, 0)
        grad_feats[:, cols(k, width)] = grad.astype(BF16)
        return carry

    lax.fori_loop(0, chunks, finish_grad, 0)
    for d in range(1, peers):
        weight_share(d).wait_recv()
    grad_self[...] = weight_all[0:narrow, :].astype(F32)
    grad_neigh[...] = weight_all[narrow:, :].astype(F32)

    for d in range(1, peers):
        slot_copy(d).wait_send()
        hub_copy(d).wait_send()
        back_copy(d).wait_send()
        hub_back_copy(d).wait_send()
        weight_copy(d).wait_send()
        weight_share(d).wait_send()

    def drain(i, carry):
        k = lax.div(i, n)
        owner = lax.rem(i, n)

        @pl.when(owner > pos)
        def _():
            right_copy(owner, k).wait_send()

        @pl.when(owner < pos)
        def _():
            left_copy(owner, k).wait_send()

        @pl.when(jnp.logical_and(owner <= pos, has_right))
        def _():
            slopes_right(owner, k).wait_send()

        @pl.when(jnp.logical_and(owner >= pos, has_left))
        def _():
            slopes_left(owner, k).wait_send()

        return carry

    lax.fori_loop(0, chunks * n, drain, 0)


def per_device(n, peers, feats, w_self, w_neigh, cotangent, loc_nbr, send_rows, recv_node, hub_rows, hub_nbr):
    narrow, nodes = feats.shape
    chunks = 4
    width = nodes // chunks
    full = w_self.shape[1]
    hubs = hub_rows.shape[0]
    every = peers * send_rows.shape[2]
    weights = jnp.concatenate([w_self, w_neigh], axis=0)
    w_turned = weights.T.reshape(n, narrow, 2 * narrow)
    lane_parts = min(peers, full // 128)
    piece = (2 * narrow * lane_parts // peers, full // lane_parts)
    vmem = pltpu.VMEM
    out = jax.ShapeDtypeStruct
    return pl.pallas_call(
        functools.partial(layer_kernel, n, peers, chunks),
        out_shape=(
            out((narrow, nodes), BF16), out((narrow, nodes), BF16),
            out((narrow, full), F32), out((narrow, full), F32),
        ),
        in_specs=[pl.BlockSpec(memory_space=vmem)] * 10,
        out_specs=[pl.BlockSpec(memory_space=vmem)] * 4,
        scratch_shapes=[
            vmem((nodes, nodes), BF16), vmem((nodes, every), BF16), vmem((nodes, every), BF16),
            vmem((peers * hubs, nodes), BF16), vmem((hubs, nodes), BF16), vmem((chunks, 16, width), F32),
            vmem((narrow, every), BF16), vmem((narrow, every), BF16),
            vmem((hubs, narrow), BF16), vmem((peers * hubs, narrow), BF16),
            vmem((chunks, narrow, width), F32), vmem((chunks, 2 * narrow, width), BF16),
            vmem((chunks, n, narrow, width), BF16), vmem((chunks, n, narrow, width), BF16),
            vmem((chunks, n, narrow, width), BF16), vmem((chunks, n, narrow, width), BF16),
            vmem((chunks, n, narrow, width), BF16),
            vmem((chunks, narrow, width), F32), vmem((narrow, nodes), BF16),
            vmem((2 * narrow, full), F32), vmem((2 * narrow, full), BF16), vmem((peers,) + piece, BF16),
            vmem(piece, BF16), vmem((2 * narrow, full), BF16),
            vmem((narrow, every), BF16), vmem((narrow, every), BF16),
            vmem((peers * hubs, narrow), F32), vmem((peers, hubs, narrow), F32),
            pltpu.SemaphoreType.DMA((6, peers)), pltpu.SemaphoreType.DMA((6, peers)),
            pltpu.SemaphoreType.DMA((2, chunks, n)), pltpu.SemaphoreType.DMA((2, chunks, n)),
            pltpu.SemaphoreType.DMA((2, chunks, n)), pltpu.SemaphoreType.DMA((2, chunks, n)),
        ],
        compiler_params=pltpu.CompilerParams(
            collective_id=0, has_side_effects=True, vmem_limit_bytes=60 * 1024 * 1024
        ),
    )(
        feats, w_self, w_neigh, w_turned, cotangent, loc_nbr.T, send_rows.reshape(1, -1),
        recv_node.reshape(1, -1), hub_rows.reshape(-1, 1), hub_nbr.T,
    )


def solution(mesh):
    return jax.shard_map(
        functools.partial(per_device, mesh.shape["col"], mesh.shape["row"]),
        mesh=mesh,
        in_specs=(
            P("col", "row"),
            P("col", None),
            P("col", None),
            P("col", "row"),
            P("row", None),
            P("row", None, None),
            P("row", None, None),
            P("row"),
            P("row", None),
        ),
        out_specs=(P("col", "row"), P("col", "row"), P("col", None), P("col", None)),
        check_vma=False,
    )
```

time: 242 us -> 142 us (0.59)
  waiting for transfers between devices: 166 us -> 0 us
  Pallas kernels: 0 us -> 131 us
  matrix products: 28.3 us -> 0 us
  between operations: 14 us -> 0.66 us
  blocking collectives: 12.7 us -> 0 us
  starting transfers between devices: 9.98 us -> 0 us
    pallas_call x0 -> x1, Pallas kernels: none -> 131 us  [per_device(): pl.pallas_call(functools.partial(layer_kernel, n, peers, chunks), out_sha...]
    psum x1 -> x0, waiting for transfers between devices: 60.6 us -> none  [per_device(): weight_total = lax.psum(dot(joined, wide, 1, 1), 'row')]
    reduce_scatter x2 -> x0, waiting for transfers between devices: 59.3 us -> none  [the longest x1 43.6 us: per_device(): lax.psum_scatter(partial, 'col', scatter_dimension=0, tiled=True)]
    all_gather x1 -> x0, waiting for transfers between devices: 45.5 us -> none  [per_device(): wide = lax.all_gather(slopes, 'col', axis=0, tiled=True)]
    dot_general x14 -> x0, matrix products: 28.3 us -> none  [dot(): lax.dot_general(a, b, (((ca,), (cb,)), ((), ())), preferred_element_type=...]
    all_gather x1 -> x0, blocking collectives: 12.7 us -> none  [per_device(): lax.all_gather(dot(own_pick, feats, 0, 1).astype(BF16), 'row', axis=0, ti...]
    all_to_all x2 -> x0, starting transfers between devices: 9.67 us -> none  [the longest x1 5.37 us: per_device(): lax.all_to_all(outgoing, 'row', split_axis=1, concat_axis=1, tiled=True)]
    slice x3 -> x0, local copies, waits for them, and re-layouts: 3.14 us -> none  [the longest x1 3.1 us: per_device(): weight_total[narrow:]]
  transfers between devices with their start and end apart: 6 -> 0, of which waited for: 4 -> 0; matrix products, arithmetic and copies ran while one was open for 8% -> 0% of each run, Pallas kernels for 0% -> 0%
where the time goes in v2:
time: 142 us; the launch traced here: 141 us
  Pallas kernels  131 us (92%)
  local copies, waits for them, and re-layouts  8.01 us (6%)
    pallas_call x1, Pallas kernels, per_device(): pl.pallas_call(functools.partial(layer_kernel, n, peers, chunks), out_sha...  131 us
    unnamed x10, local copies, waits for them, and re-layouts  5.36 us

profile of v2, /device:TPU:1, one launch (start us, length us, event | category | flops | bytes accessed | tf_op | source)
XLA Modules:
  0.0 141.0 jit_solution(13989764180951483173)
XLA Ops:
  0.6 1.3 copy.14.hub_col
  2.0 1.3 maximum_bitcast_fusion
  3.2 1.3 copy.13
  4.6 131.1 %shard_map.120 = (bf16[256,1024]{1,0:T(8,128)(2,1)}, bf16[256,1024]{1,0:T(8,128)(2,1)}, f32[256,1024]{1,0:T(8,128)}, f32[256,1024]{1,0:T(8,128)}) custom-call(bf16[256,1024]{1,0:T(8,128)(2,1)} %feats.1, bf16[256,1024]{1,0:T(8,128)(2,1)} %w_self.1, bf16[256,1024]{1,0:T(8,128)(2,1)} %w_neigh.1, bf16[4,256,512]{2,1,0:T(8,128)(2,1)} %bitcast.8, ...), custom_call_target="tpu_custom_call" | custom-call | tf_op jit(solution)/shard_map/pallas_call | solution.py:390
  135.7 0.0 copy-start.2
  135.7 0.0 copy-start.1
  135.7 2.0 %copy.19 = bf16[256,1024]{1,0:T(8,128)(2,1)} copy(bf16[256,1024]{1,0:T(8,128)(2,1)} %get-tuple-element.8) | data formatting | bytes 1048576
  137.7 0.0 copy-done.2
  137.7 0.8 copy.20
  138.5 0.0 copy-done.1
  138.5 0.0 copy-start
  138.5 1.0 copy.21
  139.4 0.6 copy-done
  140.1 1.0 copy.22
Async XLA Ops:
  135.7 2.0 %copy-start.2 = (bf16[256,1024]{1,0:T(8,128)(2,1)S(1)}, bf16[256,1024]{1,0:T(8,128)(2,1)}, u32[]{:S(2)}) copy-start(bf16[256,1024]{1,0:T(8,128)(2,1)} %get-tuple-element.9) | copy-start | bytes 1572868
  135.7 2.8 %copy-start.1 = (f32[256,1024]{1,0:T(8,128)S(1)}, f32[256,1024]{1,0:T(8,128)}, u32[]{:S(2)}) copy-start(f32[256,1024]{1,0:T(8,128)} %get-tuple-element.10) | copy-start | bytes 3145732
  138.5 1.6 %copy-start = (f32[256,1024]{1,0:T(8,128)S(1)}, f32[256,1024]{1,0:T(8,128)}, u32[]{:S(2)}) copy-start(f32[256,1024]{1,0:T(8,128)} %get-tuple-element.11) | copy-start | bytes 3145732

commit v3 on v2

--- a/solution.py
+++ b/solution.py
@@ -34,19 +34,19 @@
 
 def layer_kernel(
     n, peers, chunks,
-    feats, w_self, w_neigh, w_turned, cot, loc, send, recv, hub_col, hub,
-    hidden, grad_feats, grad_self, grad_neigh,
+    feats, w_self, w_neigh, cot, loc, send, recv, hub_row, hub,
+    hidden, grad_feats, weight_all,
     loc_pick, send_pick, recv_pick, hub_pick, own_pick, degree,
     slot_out, slot_in, hub_out, hub_in,
-    total, joined, from_left, from_right, to_left, to_right, slopes,
-    direct, share, weight_acc, weight_out, weight_in, weight_sum, weight_all,
+    w_turned, partial, total, joined, from_left, from_right, to_left, to_right, slopes,
+    direct, share, weight_acc, weight_out, weight_in, weight_sum,
     back_out, back_in, hub_back_out, hub_back_in,
     row_send, row_recv, sum_send, sum_recv, spread_send, spread_recv,
 ):
     narrow, nodes = feats.shape
     width = nodes // chunks
     slots = send.shape[1] // peers
-    hubs = hub_col.shape[0]
+    hubs = hub_row.shape[1]
     me = lax.axis_index("row")
     pos = lax.axis_index("col")
     has_left = pos > 0
@@ -108,9 +108,8 @@
         return row_copy(weight_sum, weight_all.at[rows, columns], 5, d)
 
     fill_picks(send_pick, send, 64)
-    own_rows = lax.broadcasted_iota(jnp.int32, (hubs, nodes), 1)
-    own_pick[...] = jnp.where(own_rows == hub_col[...], 1.0, 0.0).astype(BF16)
-    hub_out[...] = dot(own_pick[...], feats[...], 1, 1).astype(BF16)
+    fill_picks(own_pick, hub_row, 64)
+    hub_out[...] = dot(feats[...], own_pick[...], 1, 0).T.astype(BF16)
 
     tile = 2 * slots
 
@@ -132,14 +131,22 @@
     fill_picks(hub_pick, hub, 64)
     fixed = loc.shape[0] + hub.shape[0]
 
+    pair = 2 * width
+
     def local_part(k, carry):
-        total[k] = dot(feats[...], loc_pick[:, cols(k, width)], 1, 0)
-        joined[k, 0:narrow, :] = feats[:, cols(k, width)]
+        near = dot(feats[...], loc_pick[:, cols(k, pair)], 1, 0)
         ones = jnp.ones((16, recv_pick.shape[1]), BF16)
-        degree[k] = dot(ones, recv_pick[cols(k, width), :], 1, 1) + fixed
-        return carry
-
-    lax.fori_loop(0, chunks, local_part, 0)
+        count = dot(ones, recv_pick[cols(k, pair), :], 1, 1) + fixed
+        for half in range(2):
+            there = slice(half * width, (half + 1) * width)
+            total[2 * k + half] = near[:, there]
+            degree[2 * k + half] = count[:, there]
+            joined[2 * k + half, 0:narrow, :] = feats[:, cols(2 * k + half, width)]
+        return carry
+
+    lax.fori_loop(0, chunks // 2, local_part, 0)
+    w_turned[:, 0:narrow] = w_self[...].T
+    w_turned[:, narrow:] = w_neigh[...].T
     weight_acc[...] = jnp.zeros_like(weight_acc)
     for d in range(1, peers):
         slot_copy(d).wait_recv()
@@ -173,42 +180,46 @@
             device_id={"col": pos - 1}, device_id_type=MESH,
         )
 
-    def send_partials(k):
+    def make_partials(k):
         mean = total[k] + dot(hub_in[...], hub_pick[:, cols(k, width)], 0, 0)
         mean = mean + dot(slot_in[...], recv_pick[cols(k, width), :], 1, 1)
         joined[k, narrow:, :] = (mean / degree[k, 0:1, :]).astype(BF16)
-
+        partial[k] = dot(w_turned[...], joined[k], 1, 0).reshape(n, narrow, width)
+
+    def sums_right(k):
         def step(s, carry):
             far = n - 1 - s
 
+            @pl.when(jnp.logical_and(far > pos, has_left))
+            def _():
+                right_copy(far, k).wait_recv()
+                to_right[k, far] = (partial[k, far] + from_left[k, far].astype(F32)).astype(BF16)
+
+            @pl.when(jnp.logical_and(far > pos, jnp.logical_not(has_left)))
+            def _():
+                to_right[k, far] = partial[k, far].astype(BF16)
+
             @pl.when(far > pos)
             def _():
-                mine = dot(w_turned[far], joined[k], 1, 0)
-
-                @pl.when(has_left)
-                def _():
-                    right_copy(far, k).wait_recv()
-                    to_right[k, far] = (mine + from_left[k, far].astype(F32)).astype(BF16)
-
-                @pl.when(jnp.logical_not(has_left))
-                def _():
-                    to_right[k, far] = mine.astype(BF16)
-
                 right_copy(far, k).start()
 
+            return carry
+
+        lax.fori_loop(0, n - 1, step, 0)
+
+    def sums_left(k):
+        def step(s, carry):
+            @pl.when(jnp.logical_and(s < pos, has_right))
+            def _():
+                left_copy(s, k).wait_recv()
+                to_left[k, s] = (partial[k, s] + from_right[k, s].astype(F32)).astype(BF16)
+
+            @pl.when(jnp.logical_and(s < pos, jnp.logical_not(has_right)))
+            def _():
+                to_left[k, s] = partial[k, s].astype(BF16)
+
             @pl.when(s < pos)
             def _():
-                mine = dot(w_turned[s], joined[k], 1, 0)
-
-                @pl.when(has_right)
-                def _():
-                    left_copy(s, k).wait_recv()
-                    to_left[k, s] = (mine + from_right[k, s].astype(F32)).astype(BF16)
-
-                @pl.when(jnp.logical_not(has_right))
-                def _():
-                    to_left[k, s] = mine.astype(BF16)
-
                 left_copy(s, k).start()
 
             return carry
@@ -216,7 +227,7 @@
         lax.fori_loop(0, n - 1, step, 0)
 
     def finish_preact(k):
-        total[k] = dot(w_turned[pos], joined[k], 1, 0)
+        total[k] = partial[k, pos]
 
         @pl.when(has_left)
         def _():
@@ -243,49 +254,63 @@
 
         hidden[:, cols(k, width)] = (preact * gate).astype(BF16)
 
+    def pass_on(d, t):
+        k = t - (n - 1) - d
+        inside = jnp.logical_and(k >= 0, k < chunks)
+
+        @pl.when(jnp.logical_and(inside, pos - d >= 0))
+        def _():
+            slopes_right(pos - d, k).wait_recv()
+
+            @pl.when(has_right)
+            def _():
+                slopes_right(pos - d, k).start()
+
+        @pl.when(jnp.logical_and(inside, pos + d < n))
+        def _():
+            slopes_left(pos + d, k).wait_recv()
+
+            @pl.when(has_left)
+            def _():
+                slopes_left(pos + d, k).start()
+
     def backward(k):
-        def step(d, carry):
-            @pl.when(pos - d >= 0)
-            def _():
-                slopes_right(pos - d, k).wait_recv()
-
-                @pl.when(has_right)
-                def _():
-                    slopes_right(pos - d, k).start()
-
-            @pl.when(pos + d < n)
-            def _():
-                slopes_left(pos + d, k).wait_recv()
-
-                @pl.when(has_left)
-                def _():
-                    slopes_left(pos + d, k).start()
-
-            return carry
-
-        lax.fori_loop(1, n, step, 0)
-        wide = slopes[k].reshape(n * narrow, width)
+        wide = jnp.concatenate(
+            [slopes[k - 1].reshape(n * narrow, width), slopes[k].reshape(n * narrow, width)], axis=1
+        )
         back = dot(w_neigh[...], wide, 1, 0)
-        share[:, cols(k, width)] = (back / degree[k, 0:1, :]).astype(BF16)
-        direct[k] = dot(w_self[...], wide, 1, 0)
-        weight_acc[...] += dot(joined[k], wide, 1, 1)
+        own = dot(w_self[...], wide, 1, 0)
+        for half in range(2):
+            at = k - 1 + half
+            there = slice(half * width, (half + 1) * width)
+            share[:, cols(at, width)] = (back[:, there] / degree[at, 0:1, :]).astype(BF16)
+            direct[at] = own[:, there]
+        weight_acc[...] += dot(jnp.concatenate([joined[k - 1], joined[k]], axis=1), wide, 1, 1)
+
+    def when_inside(k, work):
+        @pl.when(jnp.logical_and(k >= 0, k < chunks))
+        def _():
+            work(k)
 
     def turn(t, carry):
-        @pl.when(t < chunks)
-        def _():
-            send_partials(t)
-
-        @pl.when(jnp.logical_and(t >= 1, t <= chunks))
-        def _():
-            finish_preact(t - 1)
-
-        @pl.when(t >= 2)
-        def _():
-            backward(t - 2)
-
-        return carry
-
-    lax.fori_loop(0, chunks + 2, turn, 0)
+        def passing(d, inner):
+            pass_on(d, t)
+            return inner
+
+        lax.fori_loop(1, n, passing, 0)
+        when_inside(t, make_partials)
+        when_inside(t - pos, sums_right)
+        when_inside(t - (n - 1 - pos), sums_left)
+        when_inside(t - (n - 1), finish_preact)
+        late = t - 2 * (n - 1)
+
+        @pl.when(jnp.logical_and(late >= 0, lax.rem(late, 2) == 1))
+        def _():
+            backward(late)
+
+        return carry
+
+    lax.fori_loop(0, chunks + 2 * (n - 1), turn, 0)
 
     def back_slots(i, carry):
         back_out[:, cols(i, tile)] = dot(share[...], recv_pick[:, cols(i, tile)], 1, 0).astype(BF16)
@@ -315,6 +340,7 @@
     hub_total = hub_back_in[0]
     for r in range(1, peers):
         hub_total = hub_total + hub_back_in[r]
+    hub_total = hub_total.T
     hub_high = hub_total.astype(BF16)
     hub_low = (hub_total - hub_high.astype(F32)).astype(BF16)
 
@@ -330,16 +356,14 @@
 
     def finish_grad(k, carry):
         grad = direct[k] + dot(back_in[...], send_pick[cols(k, width), :], 1, 1)
-        grad = grad + dot(hub_high, own_pick[:, cols(k, width)], 0, 0)
-        grad = grad + dot(hub_low, own_pick[:, cols(k, width)], 0, 0)
+        grad = grad + dot(hub_high, own_pick[cols(k, width), :], 1, 1)
+        grad = grad + dot(hub_low, own_pick[cols(k, width), :], 1, 1)
         grad_feats[:, cols(k, width)] = grad.astype(BF16)
         return carry
 
     lax.fori_loop(0, chunks, finish_grad, 0)
     for d in range(1, peers):
         weight_share(d).wait_recv()
-    grad_self[...] = weight_all[0:narrow, :].astype(F32)
-    grad_neigh[...] = weight_all[narrow:, :].astype(F32)
 
     for d in range(1, peers):
         slot_copy(d).wait_send()
@@ -376,37 +400,36 @@
 
 def per_device(n, peers, feats, w_self, w_neigh, cotangent, loc_nbr, send_rows, recv_node, hub_rows, hub_nbr):
     narrow, nodes = feats.shape
-    chunks = 4
+    chunks = 8
     width = nodes // chunks
     full = w_self.shape[1]
     hubs = hub_rows.shape[0]
     every = peers * send_rows.shape[2]
-    weights = jnp.concatenate([w_self, w_neigh], axis=0)
-    w_turned = weights.T.reshape(n, narrow, 2 * narrow)
     lane_parts = min(peers, full // 128)
     piece = (2 * narrow * lane_parts // peers, full // lane_parts)
     vmem = pltpu.VMEM
     out = jax.ShapeDtypeStruct
-    return pl.pallas_call(
+    hidden, grad_feats, weight_all = pl.pallas_call(
         functools.partial(layer_kernel, n, peers, chunks),
         out_shape=(
             out((narrow, nodes), BF16), out((narrow, nodes), BF16),
-            out((narrow, full), F32), out((narrow, full), F32),
+            out((2 * narrow, full), BF16),
         ),
-        in_specs=[pl.BlockSpec(memory_space=vmem)] * 10,
-        out_specs=[pl.BlockSpec(memory_space=vmem)] * 4,
+        in_specs=[pl.BlockSpec(memory_space=vmem)] * 9,
+        out_specs=[pl.BlockSpec(memory_space=vmem)] * 3,
         scratch_shapes=[
             vmem((nodes, nodes), BF16), vmem((nodes, every), BF16), vmem((nodes, every), BF16),
-            vmem((peers * hubs, nodes), BF16), vmem((hubs, nodes), BF16), vmem((chunks, 16, width), F32),
+            vmem((peers * hubs, nodes), BF16), vmem((nodes, hubs), BF16), vmem((chunks, 16, width), F32),
             vmem((narrow, every), BF16), vmem((narrow, every), BF16),
             vmem((hubs, narrow), BF16), vmem((peers * hubs, narrow), BF16),
+            vmem((full, 2 * narrow), BF16), vmem((chunks, n, narrow, width), F32),
             vmem((chunks, narrow, width), F32), vmem((chunks, 2 * narrow, width), BF16),
             vmem((chunks, n, narrow, width), BF16), vmem((chunks, n, narrow, width), BF16),
             vmem((chunks, n, narrow, width), BF16), vmem((chunks, n, narrow, width), BF16),
             vmem((chunks, n, narrow, width), BF16),
             vmem((chunks, narrow, width), F32), vmem((narrow, nodes), BF16),
             vmem((2 * narrow, full), F32), vmem((2 * narrow, full), BF16), vmem((peers,) + piece, BF16),
-            vmem(piece, BF16), vmem((2 * narrow, full), BF16),
+            vmem(piece, BF16),
             vmem((narrow, every), BF16), vmem((narrow, every), BF16),
             vmem((peers * hubs, narrow), F32), vmem((peers, hubs, narrow), F32),
             pltpu.SemaphoreType.DMA((6, peers)), pltpu.SemaphoreType.DMA((6, peers)),
@@ -417,9 +440,11 @@
             collective_id=0, has_side_effects=True, vmem_limit_bytes=60 * 1024 * 1024
         ),
     )(
-        feats, w_self, w_neigh, w_turned, cotangent, loc_nbr.T, send_rows.reshape(1, -1),
-        recv_node.reshape(1, -1), hub_rows.reshape(-1, 1), hub_nbr.T,
+        feats, w_self, w_neigh, cotangent, loc_nbr.T, send_rows.reshape(1, -1),
+        recv_node.reshape(1, -1), hub_rows.reshape(1, -1), hub_nbr.T,
     )
+    grads = weight_all.astype(F32)
+    return hidden, grad_feats, grads[:narrow], grads[narrow:]
 
 
 def solution(mesh):

time: 142 us -> 128 us (0.901)
  Pallas kernels: 131 us -> 122 us
  local copies, waits for them, and re-layouts: 8.01 us -> 4.85 us
    pallas_call x1, Pallas kernels: 131 us -> 122 us  [per_device(): pl.pallas_call(functools.partial(layer_kernel, n, peers, chunks), out_sha...]
    unnamed x10 -> x6, local copies, waits for them, and re-layouts: 5.36 us -> 2.03 us
    slice x0 -> x1, local copies, waits for them, and re-layouts: none -> 2.82 us  [per_device(): return (hidden, grad_feats, grads[:narrow], grads[narrow:])]
where the time goes in v3:
time: 128 us
  Pallas kernels  122 us (95%)
  local copies, waits for them, and re-layouts  4.85 us (4%)
    pallas_call x1, Pallas kernels, per_device(): pl.pallas_call(functools.partial(layer_kernel, n, peers, chunks), out_sha...  122 us
    slice x1, local copies, waits for them, and re-layouts, per_device(): return (hidden, grad_feats, grads[:narrow], grads[narrow:])  2.82 us

profile of v3, /device:TPU:1, one launch (start us, length us, event | category | flops | bytes accessed | tf_op | source)
XLA Modules:
  0.0 127.8 jit_solution(16486597360475361063)
XLA Ops:
  0.6 122.3 %shard_map.120 = (bf16[256,1024]{1,0:T(8,128)(2,1)}, bf16[256,1024]{1,0:T(8,128)(2,1)}, bf16[512,1024]{1,0:T(8,128)(2,1)}) custom-call(bf16[256,1024]{1,0:T(8,128)(2,1)} %feats.1, bf16[256,1024]{1,0:T(8,128)(2,1)} %w_self.1, bf16[256,1024]{1,0:T(8,128)(2,1)} %w_neigh.1, bf16[256,1024]{1,0:T(8,128)(2,1)} %cot.1, s32[8,1024]{1,0:T(8,128)} %bitcast.5, ...), custom_call_target="tpu_custom_call" | custom-call | tf_op jit(solution)/shard_map/pallas_call | solution.py:412
  123.0 0.0 copy-start.1
  123.0 2.8 %fusion = (f32[256,1024]{1,0:T(8,128)}, f32[256,1024]{1,0:T(8,128)}) fusion(bf16[512,1024]{1,0:T(8,128)(2,1)} %get-tuple-element.9), kind=kLoop, calls=%fused_computation | loop fusion | bytes 4194304 | tf_op jit(solution)/shard_map/slice | solution.py:447
  125.8 0.0 copy-done.1
  125.8 0.0 copy-start
  125.8 0.8 copy.15
  126.6 0.4 copy-done
  127.0 0.8 copy.16
Async XLA Ops:
  123.0 2.8 %copy-start.1 = (bf16[256,1024]{1,0:T(8,128)(2,1)S(1)}, bf16[256,1024]{1,0:T(8,128)(2,1)}, u32[]{:S(2)}) copy-start(bf16[256,1024]{1,0:T(8,128)(2,1)} %get-tuple-element.16) | copy-start | bytes 1572868
  125.8 1.2 copy-start

commit v4 on v3

--- a/solution.py
+++ b/solution.py
@@ -16,20 +16,23 @@
     return lax.dot_general(a, b, (((ca,), (cb,)), ((), ())), preferred_element_type=F32)
 
 
+def count_picks(indices, first, rows):
+    names = lax.broadcasted_iota(jnp.int32, (rows, indices.shape[1]), 0) + first
+    total = jnp.where(names == indices[0:1, :], 1.0, 0.0)
+    for k in range(1, indices.shape[0]):
+        total = total + jnp.where(names == indices[k : k + 1, :], 1.0, 0.0)
+    return total.astype(BF16)
+
+
 def fill_picks(dest, indices, strip):
-    size = dest.shape[0]
-    strip = min(strip, size)
+    strip = min(strip, dest.shape[0])
 
     def body(i, carry):
         first = pl.multiple_of(i * strip, strip)
-        rows = lax.broadcasted_iota(jnp.int32, (strip, indices.shape[1]), 0) + first
-        total = jnp.where(rows == indices[0:1, :], 1.0, 0.0)
-        for k in range(1, indices.shape[0]):
-            total = total + jnp.where(rows == indices[k : k + 1, :], 1.0, 0.0)
-        dest[pl.ds(first, strip), :] = total.astype(BF16)
-        return carry
-
-    lax.fori_loop(0, size // strip, body, 0)
+        dest[pl.ds(first, strip), :] = count_picks(indices, first, strip)
+        return carry
+
+    lax.fori_loop(0, dest.shape[0] // strip, body, 0)
 
 
 def layer_kernel(
@@ -39,7 +42,7 @@
     loc_pick, send_pick, recv_pick, hub_pick, own_pick, degree,
     slot_out, slot_in, hub_out, hub_in,
     w_turned, partial, total, joined, from_left, from_right, to_left, to_right, slopes,
-    direct, share, weight_acc, weight_out, weight_in, weight_sum,
+    direct, share, weight_acc, weight_out, twin_in, weight_half, weight_in, weight_sum,
     back_out, back_in, hub_back_out, hub_back_in,
     row_send, row_recv, sum_send, sum_recv, spread_send, spread_recv,
 ):
@@ -99,16 +102,42 @@
     def part(r):
         return cols(lax.div(r, lane_parts), part_rows), cols(lax.rem(r, lane_parts), part_cols)
 
+    chips = peers // 2
+    chip = lax.div(me, 2)
+    core = lax.rem(me, 2)
+    twin = me + 1 - 2 * core
+
+    def other_chip(d):
+        return lax.rem(chip + d, chips)
+
+    def to_row(src, dst, kind, index, peer):
+        return pltpu.make_async_remote_copy(
+            src_ref=src, dst_ref=dst, send_sem=row_send.at[kind, index], recv_sem=row_recv.at[kind, index],
+            device_id={"row": peer}, device_id_type=MESH,
+        )
+
+    def twin_copy(c):
+        rows, columns = part(2 * c + 1 - core)
+        return to_row(weight_out.at[rows, columns], twin_in.at[c], 4, c, twin)
+
     def weight_copy(d):
-        rows, columns = part(row_peer(d))
-        return row_copy(weight_out.at[rows, columns], weight_in.at[me], 4, d)
+        c = other_chip(d)
+        return to_row(weight_half.at[c], weight_in.at[chip], 5, d, 2 * c + core)
 
     def weight_share(d):
         rows, columns = part(me)
-        return row_copy(weight_sum, weight_all.at[rows, columns], 5, d)
-
-    fill_picks(send_pick, send, 64)
-    fill_picks(own_pick, hub_row, 64)
+        return to_row(weight_sum, weight_all.at[rows, columns], 6, d, 2 * other_chip(d) + core)
+
+    def weight_twin(d):
+        rows, columns = part(2 * other_chip(d) + core)
+        return to_row(weight_all.at[rows, columns], weight_all.at[rows, columns], 7, d, twin)
+
+    def weight_twin_in(d):
+        rows, columns = part(2 * other_chip(d) + 1 - core)
+        return to_row(weight_all.at[rows, columns], weight_all.at[rows, columns], 7, d, twin)
+
+    fill_picks(send_pick, send[...], 16)
+    fill_picks(own_pick, hub_row[...], 64)
     hub_out[...] = dot(feats[...], own_pick[...], 1, 0).T.astype(BF16)
 
     tile = 2 * slots
@@ -126,25 +155,34 @@
     slot_in[:, cols(me, slots)] = slot_out[:, cols(me, slots)]
     hub_in[cols(me, hubs), :] = hub_out[...]
 
-    fill_picks(loc_pick, loc, 64)
-    fill_picks(recv_pick, recv, 64)
-    fill_picks(hub_pick, hub, 64)
     fixed = loc.shape[0] + hub.shape[0]
 
-    pair = 2 * width
-
-    def local_part(k, carry):
-        near = dot(feats[...], loc_pick[:, cols(k, pair)], 1, 0)
+    def prepare(k):
+        here = cols(k, width)
+        names = loc[:, here]
+
+        def local_rows(i, carry):
+            first = pl.multiple_of(i * 128, 128)
+            loc_pick[pl.ds(first, 128), here] = count_picks(names, first, 128)
+            return carry
+
+        lax.fori_loop(0, nodes // 128, local_rows, 0)
+        targets = recv[...]
+
+        def target_rows(i, carry):
+            first = pl.multiple_of(k * width + i * 16, 16)
+            recv_pick[pl.ds(first, 16), :] = count_picks(targets, first, 16)
+            return carry
+
+        lax.fori_loop(0, width // 16, target_rows, 0)
+        hub_pick[:, here] = count_picks(hub[:, here], 0, hub_pick.shape[0])
+        total[k] = dot(feats[...], loc_pick[:, here], 1, 0)
         ones = jnp.ones((16, recv_pick.shape[1]), BF16)
-        count = dot(ones, recv_pick[cols(k, pair), :], 1, 1) + fixed
-        for half in range(2):
-            there = slice(half * width, (half + 1) * width)
-            total[2 * k + half] = near[:, there]
-            degree[2 * k + half] = count[:, there]
-            joined[2 * k + half, 0:narrow, :] = feats[:, cols(2 * k + half, width)]
-        return carry
-
-    lax.fori_loop(0, chunks // 2, local_part, 0)
+        degree[k] = dot(ones, recv_pick[here, :], 1, 1) + fixed
+        joined[k, 0:narrow, :] = feats[:, here]
+
+    prepare(0)
+    prepare(1)
     w_turned[:, 0:narrow] = w_self[...].T
     w_turned[:, narrow:] = w_neigh[...].T
     weight_acc[...] = jnp.zeros_like(weight_acc)
@@ -297,11 +335,16 @@
             pass_on(d, t)
             return inner
 
+        when_inside(t, make_partials)
         lax.fori_loop(1, n, passing, 0)
-        when_inside(t, make_partials)
         when_inside(t - pos, sums_right)
         when_inside(t - (n - 1 - pos), sums_left)
         when_inside(t - (n - 1), finish_preact)
+
+        @pl.when(t + 2 < chunks)
+        def _():
+            prepare(t + 2)
+
         late = t - 2 * (n - 1)
 
         @pl.when(jnp.logical_and(late >= 0, lax.rem(late, 2) == 1))
@@ -312,22 +355,27 @@
 
     lax.fori_loop(0, chunks + 2 * (n - 1), turn, 0)
 
+    weight_out[...] = weight_acc[...].astype(BF16)
+    for c in range(chips):
+        twin_copy(c).start()
     def back_slots(i, carry):
         back_out[:, cols(i, tile)] = dot(share[...], recv_pick[:, cols(i, tile)], 1, 0).astype(BF16)
         return carry
 
     lax.fori_loop(0, peers * slots // tile, back_slots, 0)
+    for d in range(1, peers):
+        back_copy(d).start()
     hub_back_out[...] = dot(hub_pick[...], share[...], 1, 1)
     for d in range(1, peers):
-        back_copy(d).start()
         hub_back_copy(d).start()
-    weight_out[...] = weight_acc[...].astype(BF16)
-    for d in range(1, peers):
-        weight_copy(d).start()
     back_in[:, cols(me, slots)] = back_out[:, cols(me, slots)]
     hub_back_in[me] = hub_back_out[cols(me, hubs), :]
-    my_rows, my_cols = part(me)
-    weight_in[me] = weight_out[my_rows, my_cols]
+    for c in range(chips):
+        twin_copy(c).wait_recv()
+        rows, columns = part(2 * c + core)
+        weight_half[c] = (weight_acc[rows, columns] + twin_in[c].astype(F32)).astype(BF16)
+    for d in range(1, chips):
+        weight_copy(d).start()
 
     def local_back(k, carry):
         direct[k] = direct[k] + dot(share[...], loc_pick[cols(k, width), :], 1, 1)
@@ -344,15 +392,16 @@
     hub_high = hub_total.astype(BF16)
     hub_low = (hub_total - hub_high.astype(F32)).astype(BF16)
 
-    for d in range(1, peers):
+    my_rows, my_cols = part(me)
+    sums = weight_acc[my_rows, my_cols] + twin_in[chip].astype(F32)
+    for d in range(1, chips):
         weight_copy(d).wait_recv()
-    sums = weight_in[0].astype(F32)
-    for r in range(1, peers):
-        sums = sums + weight_in[r].astype(F32)
+        sums = sums + weight_in[lax.rem(chip + chips - d, chips)].astype(F32)
     weight_sum[...] = sums.astype(BF16)
-    for d in range(1, peers):
+    for d in range(1, chips):
         weight_share(d).start()
     weight_all[my_rows, my_cols] = weight_sum[...]
+    weight_twin(0).start()
 
     def finish_grad(k, carry):
         grad = direct[k] + dot(back_in[...], send_pick[cols(k, width), :], 1, 1)
@@ -362,14 +411,24 @@
         return carry
 
     lax.fori_loop(0, chunks, finish_grad, 0)
-    for d in range(1, peers):
+    def source_chip(d):
+        return chips - d if d else 0
+
+    for d in range(1, chips):
         weight_share(d).wait_recv()
+        weight_twin(source_chip(d)).start()
+    for d in range(chips):
+        weight_twin_in(d).wait_recv()
 
     for d in range(1, peers):
         slot_copy(d).wait_send()
         hub_copy(d).wait_send()
         back_copy(d).wait_send()
         hub_back_copy(d).wait_send()
+    for d in range(chips):
+        twin_copy(d).wait_send()
+        weight_twin(d).wait_send()
+    for d in range(1, chips):
         weight_copy(d).wait_send()
         weight_share(d).wait_send()
 
@@ -428,11 +487,12 @@
             vmem((chunks, n, narrow, width), BF16), vmem((chunks, n, narrow, width), BF16),
             vmem((chunks, n, narrow, width), BF16),
             vmem((chunks, narrow, width), F32), vmem((narrow, nodes), BF16),
-            vmem((2 * narrow, full), F32), vmem((2 * narrow, full), BF16), vmem((peers,) + piece, BF16),
+            vmem((2 * narrow, full), F32), vmem((2 * narrow, full), BF16), vmem((peers // 2,) + piece, BF16),
+            vmem((peers // 2,) + piece, BF16), vmem((peers // 2,) + piece, BF16),
             vmem(piece, BF16),
             vmem((narrow, every), BF16), vmem((narrow, every), BF16),
             vmem((peers * hubs, narrow), F32), vmem((peers, hubs, narrow), F32),
-            pltpu.SemaphoreType.DMA((6, peers)), pltpu.SemaphoreType.DMA((6, peers)),
+            pltpu.SemaphoreType.DMA((8, peers)), pltpu.SemaphoreType.DMA((8, peers)),
             pltpu.SemaphoreType.DMA((2, chunks, n)), pltpu.SemaphoreType.DMA((2, chunks, n)),
             pltpu.SemaphoreType.DMA((2, chunks, n)), pltpu.SemaphoreType.DMA((2, chunks, n)),
         ],

time: 128 us -> 121 us (0.945)
  Pallas kernels: 122 us -> 115 us
    pallas_call x1, Pallas kernels: 122 us -> 115 us  [per_device(): pl.pallas_call(functools.partial(layer_kernel, n, peers, chunks), out_sha...]
where the time goes in v4:
time: 121 us; the launch traced here: 120 us
  Pallas kernels  115 us (95%)
  local copies, waits for them, and re-layouts  4.85 us (4%)
    pallas_call x1, Pallas kernels, per_device(): pl.pallas_call(functools.partial(layer_kernel, n, peers, chunks), out_sha...  115 us
    slice x1, local copies, waits for them, and re-layouts, per_device(): return (hidden, grad_feats, grads[:narrow], grads[narrow:])  2.82 us

profile of v4, /device:TPU:1, one launch (start us, length us, event | category | flops | bytes accessed | tf_op | source)
XLA Modules:
  0.0 120.4 jit_solution(14000652503897383995)
XLA Ops:
  0.6 114.9 %shard_map.120 = (bf16[256,1024]{1,0:T(8,128)(2,1)}, bf16[256,1024]{1,0:T(8,128)(2,1)}, bf16[512,1024]{1,0:T(8,128)(2,1)}) custom-call(bf16[256,1024]{1,0:T(8,128)(2,1)} %feats.1, bf16[256,1024]{1,0:T(8,128)(2,1)} %w_self.1, bf16[256,1024]{1,0:T(8,128)(2,1)} %w_neigh.1, bf16[256,1024]{1,0:T(8,128)(2,1)} %cot.1, s32[8,1024]{1,0:T(8,128)} %bitcast.5, ...), custom_call_target="tpu_custom_call" | custom-call | tf_op jit(solution)/shard_map/pallas_call | solution.py:471
  115.5 0.0 copy-start.1
  115.6 2.8 %fusion = (f32[256,1024]{1,0:T(8,128)}, f32[256,1024]{1,0:T(8,128)}) fusion(bf16[512,1024]{1,0:T(8,128)(2,1)} %get-tuple-element.9), kind=kLoop, calls=%fused_computation | loop fusion | bytes 4194304 | tf_op jit(solution)/shard_map/slice | solution.py:507
  118.4 0.0 copy-done.1
  118.4 0.0 copy-start
  118.4 0.8 copy.15
  119.2 0.4 copy-done
  119.6 0.8 copy.16
Async XLA Ops:
  115.5 2.8 %copy-start.1 = (bf16[256,1024]{1,0:T(8,128)(2,1)S(1)}, bf16[256,1024]{1,0:T(8,128)(2,1)}, u32[]{:S(2)}) copy-start(bf16[256,1024]{1,0:T(8,128)(2,1)} %get-tuple-element.16) | copy-start | bytes 1572868
  118.4 1.2 %copy-start = (bf16[256,1024]{1,0:T(8,128)(2,1)S(1)}, bf16[256,1024]{1,0:T(8,128)(2,1)}, u32[]{:S(2)}) copy-start(bf16[256,1024]{1,0:T(8,128)(2,1)} %get-tuple-element.17) | copy-start | bytes 1572868

commit v5 on v4

--- a/solution.py
+++ b/solution.py
@@ -292,25 +292,36 @@
 
         hidden[:, cols(k, width)] = (preact * gate).astype(BF16)
 
+    def turns_to_finish(owner):
+        return jnp.maximum(owner, n - 1 - owner)
+
     def pass_on(d, t):
-        k = t - (n - 1) - d
-        inside = jnp.logical_and(k >= 0, k < chunks)
-
-        @pl.when(jnp.logical_and(inside, pos - d >= 0))
-        def _():
-            slopes_right(pos - d, k).wait_recv()
+        def due(owner):
+            k = t - turns_to_finish(owner) - d
+            inside = jnp.logical_and(owner >= 0, owner < n)
+            return k, jnp.logical_and(inside, jnp.logical_and(k >= 0, k < chunks))
+
+        left_owner = pos - d
+        k_left, due_left = due(left_owner)
+
+        @pl.when(due_left)
+        def _():
+            slopes_right(left_owner, k_left).wait_recv()
 
             @pl.when(has_right)
             def _():
-                slopes_right(pos - d, k).start()
-
-        @pl.when(jnp.logical_and(inside, pos + d < n))
-        def _():
-            slopes_left(pos + d, k).wait_recv()
+                slopes_right(left_owner, k_left).start()
+
+        right_owner = pos + d
+        k_right, due_right = due(right_owner)
+
+        @pl.when(due_right)
+        def _():
+            slopes_left(right_owner, k_right).wait_recv()
 
             @pl.when(has_left)
             def _():
-                slopes_left(pos + d, k).start()
+                slopes_left(right_owner, k_right).start()
 
     def backward(k):
         wide = jnp.concatenate(
@@ -336,15 +347,15 @@
             return inner
 
         when_inside(t, make_partials)
-        lax.fori_loop(1, n, passing, 0)
         when_inside(t - pos, sums_right)
         when_inside(t - (n - 1 - pos), sums_left)
-        when_inside(t - (n - 1), finish_preact)
+        when_inside(t - turns_to_finish(pos), finish_preact)
 
         @pl.when(t + 2 < chunks)
         def _():
             prepare(t + 2)
 
+        lax.fori_loop(1, n, passing, 0)
         late = t - 2 * (n - 1)
 
         @pl.when(jnp.logical_and(late >= 0, lax.rem(late, 2) == 1))

time: 121 us -> 108 us (0.89)
  Pallas kernels: 115 us -> 102 us
    pallas_call x1, Pallas kernels: 115 us -> 102 us  [per_device(): pl.pallas_call(functools.partial(layer_kernel, n, peers, chunks), out_sha...]
where the time goes in v5:
time: 108 us
  Pallas kernels  102 us (94%)
  local copies, waits for them, and re-layouts  4.85 us (4%)
    pallas_call x1, Pallas kernels, per_device(): pl.pallas_call(functools.partial(layer_kernel, n, peers, chunks), out_sha...  102 us
    slice x1, local copies, waits for them, and re-layouts, per_device(): return (hidden, grad_feats, grads[:narrow], grads[narrow:])  2.82 us

profile of v5, /device:TPU:1, one launch (start us, length us, event | category | flops | bytes accessed | tf_op | source)
XLA Modules:
  0.0 107.5 jit_solution(17223878147625916852)
XLA Ops:
  0.6 102.0 %shard_map.120 = (bf16[256,1024]{1,0:T(8,128)(2,1)}, bf16[256,1024]{1,0:T(8,128)(2,1)}, bf16[512,1024]{1,0:T(8,128)(2,1)}) custom-call(bf16[256,1024]{1,0:T(8,128)(2,1)} %feats.1, bf16[256,1024]{1,0:T(8,128)(2,1)} %w_self.1, bf16[256,1024]{1,0:T(8,128)(2,1)} %w_neigh.1, bf16[256,1024]{1,0:T(8,128)(2,1)} %cot.1, s32[8,1024]{1,0:T(8,128)} %bitcast.5, ...), custom_call_target="tpu_custom_call" | custom-call | tf_op jit(solution)/shard_map/pallas_call | solution.py:482
  102.7 0.0 copy-start.1
  102.7 2.8 %fusion = (f32[256,1024]{1,0:T(8,128)}, f32[256,1024]{1,0:T(8,128)}) fusion(bf16[512,1024]{1,0:T(8,128)(2,1)} %get-tuple-element.9), kind=kLoop, calls=%fused_computation | loop fusion | bytes 4194304 | tf_op jit(solution)/shard_map/slice | solution.py:518
  105.5 0.0 copy-done.1
  105.5 0.0 copy-start
  105.5 0.8 copy.15
  106.3 0.4 copy-done
  106.7 0.8 copy.16
Async XLA Ops:
  102.7 2.8 %copy-start.1 = (bf16[256,1024]{1,0:T(8,128)(2,1)S(1)}, bf16[256,1024]{1,0:T(8,128)(2,1)}, u32[]{:S(2)}) copy-start(bf16[256,1024]{1,0:T(8,128)(2,1)} %get-tuple-element.16) | copy-start | bytes 1572868
  105.5 1.2 %copy-start = (bf16[256,1024]{1,0:T(8,128)(2,1)S(1)}, bf16[256,1024]{1,0:T(8,128)(2,1)}, u32[]{:S(2)}) copy-start(bf16[256,1024]{1,0:T(8,128)(2,1)} %get-tuple-element.17) | copy-start | bytes 1572868

commit v6 on v5

--- a/solution.py
+++ b/solution.py
@@ -38,11 +38,11 @@
 def layer_kernel(
     n, peers, chunks,
     feats, w_self, w_neigh, cot, loc, send, recv, hub_row, hub,
-    hidden, grad_feats, weight_all,
+    hidden, grad_feats, grad_self, grad_neigh,
     loc_pick, send_pick, recv_pick, hub_pick, own_pick, degree,
     slot_out, slot_in, hub_out, hub_in,
     w_turned, partial, total, joined, from_left, from_right, to_left, to_right, slopes,
-    direct, share, weight_acc, weight_out, twin_in, weight_half, weight_in, weight_sum,
+    direct, share, weight_acc, weight_out, twin_in, weight_half, weight_in, weight_sum, weight_all,
     back_out, back_in, hub_back_out, hub_back_in,
     row_send, row_recv, sum_send, sum_recv, spread_send, spread_recv,
 ):
@@ -136,23 +136,31 @@
         rows, columns = part(2 * other_chip(d) + 1 - core)
         return to_row(weight_all.at[rows, columns], weight_all.at[rows, columns], 7, d, twin)
 
-    fill_picks(send_pick, send[...], 16)
     fill_picks(own_pick, hub_row[...], 64)
     hub_out[...] = dot(feats[...], own_pick[...], 1, 0).T.astype(BF16)
 
-    tile = 2 * slots
-
-    def gather_out(i, carry):
-        slot_out[:, cols(i, tile)] = dot(feats[...], send_pick[:, cols(i, tile)], 1, 0).astype(BF16)
-        return carry
-
-    lax.fori_loop(0, peers * slots // tile, gather_out, 0)
+    def gather_for(peer):
+        here = cols(peer, slots)
+        names = send[:, here]
+
+        def rows(i, carry):
+            first = pl.multiple_of(i * 128, 128)
+            send_pick[pl.ds(first, 128), here] = count_picks(names, first, 128)
+            return carry
+
+        lax.fori_loop(0, nodes // 128, rows, 0)
+        return dot(feats[...], send_pick[:, here], 1, 0).astype(BF16)
 
     pl.semaphore_wait(barrier, peers - 1 + has_left.astype(jnp.int32) + has_right.astype(jnp.int32))
-    for d in range(1, peers):
+
+    def gather_and_send(d, carry):
+        slot_out[:, cols(row_peer(d), slots)] = gather_for(row_peer(d))
         slot_copy(d).start()
         hub_copy(d).start()
-    slot_in[:, cols(me, slots)] = slot_out[:, cols(me, slots)]
+        return carry
+
+    lax.fori_loop(1, peers, gather_and_send, 0)
+    slot_in[:, cols(me, slots)] = gather_for(me)
     hub_in[cols(me, hubs), :] = hub_out[...]
 
     fixed = loc.shape[0] + hub.shape[0]
@@ -369,24 +377,27 @@
     weight_out[...] = weight_acc[...].astype(BF16)
     for c in range(chips):
         twin_copy(c).start()
-    def back_slots(i, carry):
-        back_out[:, cols(i, tile)] = dot(share[...], recv_pick[:, cols(i, tile)], 1, 0).astype(BF16)
-        return carry
-
-    lax.fori_loop(0, peers * slots // tile, back_slots, 0)
-    for d in range(1, peers):
+    def back_slots(peer):
+        return dot(share[...], recv_pick[:, cols(peer, slots)], 1, 0).astype(BF16)
+
+    def back_and_send(d, carry):
+        back_out[:, cols(row_peer(d), slots)] = back_slots(row_peer(d))
         back_copy(d).start()
+        return carry
+
+    lax.fori_loop(1, peers, back_and_send, 0)
     hub_back_out[...] = dot(hub_pick[...], share[...], 1, 1)
     for d in range(1, peers):
         hub_back_copy(d).start()
-    back_in[:, cols(me, slots)] = back_out[:, cols(me, slots)]
+    back_in[:, cols(me, slots)] = back_slots(me)
     hub_back_in[me] = hub_back_out[cols(me, hubs), :]
-    for c in range(chips):
+    for d in range(1, chips):
+        c = other_chip(d)
         twin_copy(c).wait_recv()
         rows, columns = part(2 * c + core)
         weight_half[c] = (weight_acc[rows, columns] + twin_in[c].astype(F32)).astype(BF16)
-    for d in range(1, chips):
         weight_copy(d).start()
+    twin_copy(chip).wait_recv()
 
     def local_back(k, carry):
         direct[k] = direct[k] + dot(share[...], loc_pick[cols(k, width), :], 1, 1)
@@ -430,6 +441,8 @@
         weight_twin(source_chip(d)).start()
     for d in range(chips):
         weight_twin_in(d).wait_recv()
+    grad_self[...] = weight_all[0:narrow, :]
+    grad_neigh[...] = weight_all[narrow:, :]
 
     for d in range(1, peers):
         slot_copy(d).wait_send()
@@ -479,14 +492,14 @@
     piece = (2 * narrow * lane_parts // peers, full // lane_parts)
     vmem = pltpu.VMEM
     out = jax.ShapeDtypeStruct
-    hidden, grad_feats, weight_all = pl.pallas_call(
+    hidden, grad_feats, grad_self, grad_neigh = pl.pallas_call(
         functools.partial(layer_kernel, n, peers, chunks),
         out_shape=(
             out((narrow, nodes), BF16), out((narrow, nodes), BF16),
-            out((2 * narrow, full), BF16),
+            out((narrow, full), BF16), out((narrow, full), BF16),
         ),
         in_specs=[pl.BlockSpec(memory_space=vmem)] * 9,
-        out_specs=[pl.BlockSpec(memory_space=vmem)] * 3,
+        out_specs=[pl.BlockSpec(memory_space=vmem)] * 4,
         scratch_shapes=[
             vmem((nodes, nodes), BF16), vmem((nodes, every), BF16), vmem((nodes, every), BF16),
             vmem((peers * hubs, nodes), BF16), vmem((nodes, hubs), BF16), vmem((chunks, 16, width), F32),
@@ -500,7 +513,7 @@
             vmem((chunks, narrow, width), F32), vmem((narrow, nodes), BF16),
             vmem((2 * narrow, full), F32), vmem((2 * narrow, full), BF16), vmem((peers // 2,) + piece, BF16),
             vmem((peers // 2,) + piece, BF16), vmem((peers // 2,) + piece, BF16),
-            vmem(piece, BF16),
+            vmem(piece, BF16), vmem((2 * narrow, full), BF16),
             vmem((narrow, every), BF16), vmem((narrow, every), BF16),
             vmem((peers * hubs, narrow), F32), vmem((peers, hubs, narrow), F32),
             pltpu.SemaphoreType.DMA((8, peers)), pltpu.SemaphoreType.DMA((8, peers)),
@@ -514,8 +527,7 @@
         feats, w_self, w_neigh, cotangent, loc_nbr.T, send_rows.reshape(1, -1),
         recv_node.reshape(1, -1), hub_rows.reshape(1, -1), hub_nbr.T,
     )
-    grads = weight_all.astype(F32)
-    return hidden, grad_feats, grads[:narrow], grads[narrow:]
+    return hidden, grad_feats, grad_self.astype(F32), grad_neigh.astype(F32)
 
 
 def solution(mesh):

time: 108 us -> 108 us (level)
  other arithmetic: 0 us -> 3.27 us
  local copies, waits for them, and re-layouts: 4.85 us -> 2.03 us
    convert_element_type x0 -> x2, other arithmetic: none -> 3.27 us  [per_device(): return (hidden, grad_feats, grad_self.astype(F32), grad_neigh.astype(F32))]
    slice x1 -> x0, local copies, waits for them, and re-layouts: 2.82 us -> none  [per_device(): return (hidden, grad_feats, grads[:narrow], grads[narrow:])]
where the time goes in v6:
time: 108 us
  Pallas kernels  102 us (94%)
  other arithmetic  3.27 us (3%)
  local copies, waits for them, and re-layouts  2.03 us (2%)
    pallas_call x1, Pallas kernels, per_device(): pl.pallas_call(functools.partial(layer_kernel, n, peers, chunks), out_sha...  102 us
    convert_element_type x2, other arithmetic, per_device(): return (hidden, grad_feats, grad_self.astype(F32), grad_neigh.astype(F32))  3.27 us

profile of v6, /device:TPU:1, one launch (start us, length us, event | category | flops | bytes accessed | tf_op | source)
XLA Modules:
  0.0 107.7 jit_solution(17004907380946817716)
XLA Ops:
  0.6 101.8 %shard_map.120 = (bf16[256,1024]{1,0:T(8,128)(2,1)}, bf16[256,1024]{1,0:T(8,128)(2,1)}, bf16[256,1024]{1,0:T(8,128)(2,1)}, bf16[256,1024]{1,0:T(8,128)(2,1)}) custom-call(bf16[256,1024]{1,0:T(8,128)(2,1)} %feats.1, bf16[256,1024]{1,0:T(8,128)(2,1)} %w_self.1, bf16[256,1024]{1,0:T(8,128)(2,1)} %w_neigh.1, bf16[256,1024]{1,0:T(8,128)(2,1)} %cot.1, ...), custom_call_target="tpu_custom_call" | custom-call | tf_op jit(solution)/shard_map/pallas_call | solution.py:495
  102.4 0.0 copy-start
  102.4 2.2 %convert_element_type.6 = f32[256,1024]{1,0:T(8,128)} convert(bf16[256,1024]{1,0:T(8,128)(2,1)} %get-tuple-element.10) | non-fusion elementwise | flops 262144 | bytes 1572864 | tf_op jit(solution)/shard_map/convert_element_type | solution.py:530
  104.6 0.0 copy-done
  104.6 0.0 copy-start.2
  104.6 1.1 %convert_element_type.7 = f32[256,1024]{1,0:T(8,128)} convert(bf16[256,1024]{1,0:T(8,128)(2,1)S(1)} %copy-done) | non-fusion elementwise | flops 262144 | bytes 1572864 | tf_op jit(solution)/shard_map/convert_element_type | solution.py:530
  105.7 0.0 copy-done.2
  105.7 0.0 copy-start.1
  105.7 0.8 copy.15
  106.5 0.4 copy-done.1
  106.9 0.8 copy.16
Async XLA Ops:
  102.4 2.2 %copy-start = (bf16[256,1024]{1,0:T(8,128)(2,1)S(1)}, bf16[256,1024]{1,0:T(8,128)(2,1)}, u32[]{:S(2)}) copy-start(bf16[256,1024]{1,0:T(8,128)(2,1)} %get-tuple-element.11) | copy-start | bytes 1572868
  104.6 1.1 %copy-start.2 = (bf16[256,1024]{1,0:T(8,128)(2,1)S(1)}, bf16[256,1024]{1,0:T(8,128)(2,1)}, u32[]{:S(2)}) copy-start(bf16[256,1024]{1,0:T(8,128)(2,1)} %get-tuple-element.16) | copy-start | bytes 1572868
  105.7 1.2 %copy-start.1 = (bf16[256,1024]{1,0:T(8,128)(2,1)S(1)}, bf16[256,1024]{1,0:T(8,128)(2,1)}, u32[]{:S(2)}) copy-start(bf16[256,1024]{1,0:T(8,128)(2,1)} %get-tuple-element.17) | copy-start | bytes 1572868

commit v7 on v5

--- a/solution.py
+++ b/solution.py
@@ -182,7 +182,6 @@
         joined[k, 0:narrow, :] = feats[:, here]
 
     prepare(0)
-    prepare(1)
     w_turned[:, 0:narrow] = w_self[...].T
     w_turned[:, narrow:] = w_neigh[...].T
     weight_acc[...] = jnp.zeros_like(weight_acc)
@@ -351,9 +350,9 @@
         when_inside(t - (n - 1 - pos), sums_left)
         when_inside(t - turns_to_finish(pos), finish_preact)
 
-        @pl.when(t + 2 < chunks)
-        def _():
-            prepare(t + 2)
+        @pl.when(t + 1 < chunks)
+        def _():
+            prepare(t + 1)
 
         lax.fori_loop(1, n, passing, 0)
         late = t - 2 * (n - 1)
@@ -381,12 +380,13 @@
         hub_back_copy(d).start()
     back_in[:, cols(me, slots)] = back_out[:, cols(me, slots)]
     hub_back_in[me] = hub_back_out[cols(me, hubs), :]
-    for c in range(chips):
+    for d in range(1, chips):
+        c = other_chip(d)
         twin_copy(c).wait_recv()
         rows, columns = part(2 * c + core)
         weight_half[c] = (weight_acc[rows, columns] + twin_in[c].astype(F32)).astype(BF16)
-    for d in range(1, chips):
         weight_copy(d).start()
+    twin_copy(chip).wait_recv()
 
     def local_back(k, carry):
         direct[k] = direct[k] + dot(share[...], loc_pick[cols(k, width), :], 1, 1)

time: 108 us -> 108 us (level)
  no operation moved by 1% of the time
where the time goes in v7:
time: 108 us
  Pallas kernels  102 us (94%)
  local copies, waits for them, and re-layouts  4.85 us (4%)
    pallas_call x1, Pallas kernels, per_device(): pl.pallas_call(functools.partial(layer_kernel, n, peers, chunks), out_sha...  102 us
    slice x1, local copies, waits for them, and re-layouts, per_device(): return (hidden, grad_feats, grads[:narrow], grads[narrow:])  2.82 us

profile of v7, /device:TPU:1, one launch (start us, length us, event | category | flops | bytes accessed | tf_op | source)
XLA Modules:
  0.0 107.5 jit_solution(3190028287429331005)
XLA Ops:
  0.6 102.0 %shard_map.120 = (bf16[256,1024]{1,0:T(8,128)(2,1)}, bf16[256,1024]{1,0:T(8,128)(2,1)}, bf16[512,1024]{1,0:T(8,128)(2,1)}) custom-call(bf16[256,1024]{1,0:T(8,128)(2,1)} %feats.1, bf16[256,1024]{1,0:T(8,128)(2,1)} %w_self.1, bf16[256,1024]{1,0:T(8,128)(2,1)} %w_neigh.1, bf16[256,1024]{1,0:T(8,128)(2,1)} %cot.1, s32[8,1024]{1,0:T(8,128)} %bitcast.5, ...), custom_call_target="tpu_custom_call" | custom-call | tf_op jit(solution)/shard_map/pallas_call | solution.py:482
  102.7 0.0 copy-start.1
  102.7 2.8 %fusion = (f32[256,1024]{1,0:T(8,128)}, f32[256,1024]{1,0:T(8,128)}) fusion(bf16[512,1024]{1,0:T(8,128)(2,1)} %get-tuple-element.9), kind=kLoop, calls=%fused_computation | loop fusion | bytes 4194304 | tf_op jit(solution)/shard_map/slice | solution.py:518
  105.5 0.0 copy-done.1
  105.5 0.0 copy-start
  105.5 0.8 copy.15
  106.3 0.4 copy-done
  106.7 0.8 copy.16
Async XLA Ops:
  102.7 2.8 %copy-start.1 = (bf16[256,1024]{1,0:T(8,128)(2,1)S(1)}, bf16[256,1024]{1,0:T(8,128)(2,1)}, u32[]{:S(2)}) copy-start(bf16[256,1024]{1,0:T(8,128)(2,1)} %get-tuple-element.16) | copy-start | bytes 1572868
  105.5 1.2 %copy-start = (bf16[256,1024]{1,0:T(8,128)(2,1)S(1)}, bf16[256,1024]{1,0:T(8,128)(2,1)}, u32[]{:S(2)}) copy-start(bf16[256,1024]{1,0:T(8,128)(2,1)} %get-tuple-element.17) | copy-start | bytes 1572868
